TPU v7x, 32 devices: a whole 2x2x4 slice. The times are simulated.
32 devices in a mesh: groups: 2 (over y), scan: 4 (over x, core), tile: 4 (over z).
Axes of the slice: x: 2, y: 2, z: 4, core: 2. Of those that a mesh axis runs over, the one named last changes fastest.
Arguments:
- object_field: float32 [2, 1024, 2048], P(None, ('groups', 'scan'), 'tile'), parts along dimension 1, may hold values from -5 to 5
- probe: float32 [16, 2, 256, 256], P('groups'), parts along dimension 0, may hold values from -1.5 to 1.5
- measured: float32 [32, 256, 256], P(('groups', 'scan', 'tile')), parts along dimension 0, may hold values from 0 to 1
- positions: int32 [32, 2], P('groups'), parts along dimension 0, may hold values from 0 to 1792, as said below
Outputs:
- object_gradient: float32 [2, 1024, 2048], P(None, ('groups', 'scan'), 'tile'), parts along dimension 1
- probe_gradient: float32 [16, 2, 256, 256], P(('groups', 'tile')), parts along dimension 0
There are 2 independent parts, one for each index of `groups`. A program takes and returns all parts, laid end to end along the dimension named above; each array names one. Nothing has to cross between parts.
Inputs may be any that keep to these rules, and one draw needn't show every extreme that they name: `positions`: each row lies in 0 to 256 and each column in 0 to 1792, so every patch lies inside the object; some patch touches the top, the bottom and the right edge.
All inputs are finite; a program needn't handle non-finite values.
Results may differ from a plain program's by a relative error of at most 0.0003.
Values sent between devices are 32-bit elements; how exact they have to be, the bound alone decides.
A program may use at most 128 MiB of HBM per device.

v0:
```python
import math

import jax
import jax.numpy as jnp
from jax import lax
from jax.sharding import PartitionSpec as P


def dft_tables(length):
    steps = lax.iota(jnp.int32, length)
    product = steps[:, None] * steps[None, :] % length
    angle = product.astype(jnp.float32) * (2.0 * math.pi / length)
    factor = 1.0 / math.sqrt(length)
    return (jnp.cos(angle) * factor, -jnp.sin(angle) * factor)


def transform(real_part, imag_part, cos_table, sin_table):
    highest = lax.Precision.HIGHEST
    left_re = jnp.einsum("uv,pmvw->pmuw", cos_table, real_part, precision=highest) - jnp.einsum(
        "uv,pmvw->pmuw", sin_table, imag_part, precision=highest
    )
    left_im = jnp.einsum("uv,pmvw->pmuw", cos_table, imag_part, precision=highest) + jnp.einsum(
        "uv,pmvw->pmuw", sin_table, real_part, precision=highest
    )
    out_re = jnp.einsum("pmuv,vw->pmuw", left_re, cos_table, precision=highest) - jnp.einsum(
        "pmuv,vw->pmuw", left_im, sin_table, precision=highest
    )
    out_im = jnp.einsum("pmuv,vw->pmuw", left_re, sin_table, precision=highest) + jnp.einsum(
        "pmuv,vw->pmuw", left_im, cos_table, precision=highest
    )
    return (out_re, out_im)


def body(object_field, probe, measured, positions):
    strip_rows = object_field.shape[1]
    tile_cols = object_field.shape[2]
    pattern_count = measured.shape[0]
    edge_len = measured.shape[1]
    mode_count = probe.shape[0]
    scan_count = lax.axis_size("scan")
    tile_count = lax.axis_size("tile")
    scan_index = lax.axis_index("scan")
    tile_index = lax.axis_index("tile")
    total_rows = strip_rows * scan_count
    anchor = jnp.zeros((), jnp.int32)
    column_pos = lax.dynamic_index_in_dim(
        positions.reshape(scan_count, tile_count, pattern_count, 2),
        tile_index,
        axis=1,
        keepdims=False,
    )
    own_pos = lax.dynamic_index_in_dim(column_pos, scan_index, axis=0, keepdims=False)
    strip = lax.all_gather(object_field, "tile", axis=2, tiled=True)
    strip_top = scan_index * strip_rows

    def cut_slice(position):
        row_at = position[0]
        block_piece = lax.dynamic_slice(
            strip, (anchor, anchor, position[1]), (2, strip_rows, edge_len)
        )
        intersections = jnp.logical_and(
            strip_top < row_at + edge_len, strip_top + strip_rows > row_at
        )
        return jnp.where(intersections, block_piece, 0.0)

    outgoing = jax.vmap(jax.vmap(cut_slice), out_axes=2)(column_pos)
    incoming = lax.all_to_all(outgoing, "scan", split_axis=2, concat_axis=2, tiled=True)
    columns = incoming.reshape(pattern_count, 2, total_rows, edge_len)

    def take_patch(column, position):
        return lax.dynamic_slice(column, (anchor, position[0], anchor), (2, edge_len, edge_len))

    patches = jax.vmap(take_patch)(columns, own_pos)
    patch_re = patches[:, 0][:, None]
    patch_im = patches[:, 1][:, None]
    probe_re = probe[:, 0][None]
    probe_im = probe[:, 1][None]
    exit_re = probe_re * patch_re - probe_im * patch_im
    exit_im = probe_re * patch_im + probe_im * patch_re
    cos_table, sin_table = dft_tables(edge_len)
    far_re, far_im = transform(exit_re, exit_im, cos_table, sin_table)
    model_int = jnp.sum(far_re * far_re + far_im * far_im, axis=1)
    weight = (2.0 * (model_int - measured))[:, None]
    back_re, back_im = transform(weight * far_re, weight * far_im, cos_table, -sin_table)
    numer_re = jnp.sum(probe_re * back_re + probe_im * back_im, axis=1)
    numer_im = jnp.sum(probe_re * back_im - probe_im * back_re, axis=1)
    probe_power = jnp.sum(probe[:, 0] * probe[:, 0] + probe[:, 1] * probe[:, 1], axis=0)
    grad_images = jnp.stack(
        [numer_re, numer_im, jnp.broadcast_to(probe_power, numer_re.shape)], axis=1
    )

    def place_image(grad_image, position):
        blank = jnp.zeros((3, total_rows, edge_len), jnp.float32)
        return lax.dynamic_update_slice(blank, grad_image, (anchor, position[0], anchor))

    placed = jax.vmap(place_image)(grad_images, own_pos).reshape(
        pattern_count, 3, scan_count, strip_rows, edge_len
    )
    returned = lax.all_to_all(placed, "scan", split_axis=2, concat_axis=2, tiled=True)
    strip_grad = jnp.zeros((3, strip_rows, tile_cols * tile_count), jnp.float32)
    slot_rows = returned[0]

    def add_piece(source, strip_acc):
        col_at = column_pos[source, 0, 1]
        block_piece = lax.dynamic_index_in_dim(slot_rows, source, axis=1, keepdims=False)
        window = lax.dynamic_slice(strip_acc, (anchor, anchor, col_at), (3, strip_rows, edge_len))
        return lax.dynamic_update_slice(strip_acc, window + block_piece, (anchor, anchor, col_at))

    strip_grad = lax.fori_loop(0, scan_count, add_piece, strip_grad)
    summed_tile = lax.psum_scatter(strip_grad, "tile", scatter_dimension=2, tiled=True)
    object_gradient = summed_tile[:2] / jnp.maximum(summed_tile[2], 1.0)[None]
    probe_numer = jnp.stack(
        [
            jnp.sum(patch_re * back_re + patch_im * back_im, axis=0),
            jnp.sum(patch_re * back_im - patch_im * back_re, axis=0),
        ],
        axis=1,
    )
    probe_weight = jnp.sum(patches[:, 0] * patches[:, 0] + patches[:, 1] * patches[:, 1], axis=0)
    per_tile = mode_count // tile_count
    numer_all, weight_all = lax.psum((probe_numer, probe_weight), ("scan", "tile"))
    own_modes = lax.dynamic_slice_in_dim(numer_all, tile_index * per_tile, per_tile, 0)
    probe_gradient = own_modes / (weight_all + 1e-05)[None, None]
    return (object_gradient, probe_gradient)


def solution(mesh):
    return jax.shard_map(
        body,
        mesh=mesh,
        in_specs=(
            P(None, ("groups", "scan"), "tile"),
            P("groups", None, None, None),
            P(("groups", "scan", "tile"), None, None),
            P("groups", None),
        ),
        out_specs=(P(None, ("groups", "scan"), "tile"), P(("groups", "tile"), None, None, None)),
        check_vma=False,
    )
```

profile of v0, /device:TPU:13, one launch (start us, length us, event | category | flops | bytes accessed | tf_op | source)
XLA Modules:
  0.0 344.1 jit_solution(9161361470429641448)
XLA Ops:
  10.6 44.7 %all-gather.2.cloned.1.call-done = f32[2,128,2048]{1,0,2:T(2,128)} async-done(((f32[2,128,512]{1,0,2:T(2,128)}), f32[2,128,2048]{1,0,2:T(2,128)}) %all-gather.2.cloned.1.call-update) | async-done | bytes 2097168 | tf_op jit(solution)/shard_map/all_gather | solution.py:53
  64.9 13.3 %all-to-all-done = f32[1,2,4,128,256]{3,1,4,0,2:T(2,128)S(1)} async-done(((f32[1,2,4,128,256]{3,1,4,0,2:T(2,128)}), f32[1,2,4,128,256]{3,1,4,0,2:T(2,128)S(1)}, u32[]{:S(2)}, u32[]{:S(2)}) %all-to-all-start) | async-done | bytes 1048608 | tf_op jit(solution)/shard_map/all_to_all | solution.py:67
  79.6 6.9 %fusion.77 = f32[8,256,256]{2,1,0:T(8,128)S(1)} fusion(f32[8,2,256,256]{3,2,1,0:T(8,128)} %param.9, f32[256,256]{1,0:T(8,128)S(1)} %get-tuple-element.130, f32[256,256]{1,0:T(8,128)S(1)} %get-tuple-element.129), kind=kOutput, calls=%fused_computation.95 | convolution fusion | flops 1613168640 | bytes 6815744 | tf_op jit(solution)/shard_map/uv,pmvw->pmuw/dot_general | solution.py:19
  86.5 4.5 %fusion.74 = f32[8,256,256]{2,1,0:T(8,128)S(1)} fusion(f32[8,2,256,256]{3,2,1,0:T(8,128)S(1)} %copy-done, f32[256,256]{1,0:T(8,128)S(1)} %get-tuple-element.130, f32[256,256]{1,0:T(8,128)S(1)} %get-tuple-element.129), kind=kOutput, calls=%fused_computation.92 | convolution fusion | flops 1613168640 | bytes 6815744 | tf_op jit(solution)/shard_map/uv,pmvw->pmuw/dot_general | solution.py:22
  91.1 4.6 %convolution_add_fusion = f32[8,256,256]{2,1,0:T(8,128)S(1)} fusion(f32[8,256,256]{2,1,0:T(8,128)S(1)} %fusion.74, f32[8,2,256,256]{3,2,1,0:T(8,128)S(1)} %copy-done, f32[256,256]{1,0:T(8,128)S(1)} %get-tuple-element.130, f32[256,256]{1,0:T(8,128)S(1)} %get-tuple-element.129), kind=kOutput, calls=%fused_computation.55 | convolution fusion | flops 1613758464 | bytes 8912896 | tf_op jit(solution)/shard_map/uv,pmvw->pmuw/dot_general | solution.py:22
  95.7 4.4 %fusion.18 = f32[8,256,256]{2,1,0:T(8,128)S(1)} fusion(f32[8,256,256]{2,1,0:T(8,128)S(1)} %convolution_add_fusion), kind=kOutput, calls=%fused_computation.32 | convolution fusion | flops 1611661312 | bytes 4194304 | tf_op jit(solution)/shard_map/pmuv,vw->pmuw/dot_general | solution.py:25
  104.6 4.8 %convolution_subtract_fusion = f32[8,256,256]{2,1,0:T(8,128)S(1)} fusion(f32[8,256,256]{2,1,0:T(8,128)S(1)} %fusion.77, f32[8,2,256,256]{3,2,1,0:T(8,128)S(1)} %copy-done, f32[256,256]{1,0:T(8,128)S(1)} %get-tuple-element.130, f32[256,256]{1,0:T(8,128)S(1)} %get-tuple-element.129), kind=kOutput, calls=%fused_computation.56 | convolution fusion | flops 1613758464 | bytes 8912896 | tf_op jit(solution)/shard_map/uv,pmvw->pmuw/dot_general | solution.py:19
  109.4 4.4 %fusion.38 = f32[8,256,256]{2,1,0:T(8,128)S(1)} fusion(f32[8,256,256]{2,1,0:T(8,128)S(1)} %fusion.18, f32[8,256,256]{2,1,0:T(8,128)S(1)} %convolution_subtract_fusion), kind=kOutput, calls=%fused_computation.51 | convolution fusion | flops 1612120064 | bytes 6291456 | tf_op jit(solution)/shard_map/pmuv,vw->pmuw/dot_general | solution.py:25
  113.9 4.6 %add_reduce_fusion = (f32[256,256]{1,0:T(8,128)S(1)}, f32[8,256,256]{2,1,0:T(8,128)S(1)}) fusion(f32[8,256,256]{2,1,0:T(8,128)S(1)} %fusion.38, f32[8,256,256]{2,1,0:T(8,128)S(1)} %fusion.16, f32[8,256,256]{2,1,0:T(8,128)S(1)} %convolution_subtract_fusion), kind=kOutput, calls=%fused_computation.40 | convolution fusion | flops 1614217216 | bytes 8650752 | tf_op jit(solution)/shard_map/pmuv,vw->pmuw/dot_general | solution.py:28
  118.5 4.6 %fusion.26 = f32[8,256,256]{2,1,0:T(8,128)S(1)} fusion(f32[8,256,256]{2,1,0:T(8,128)S(1)} %get-tuple-element.140, f32[256,256]{1,0:T(8,128)S(1)} %fusion.64), kind=kOutput, calls=%fused_computation.43 | convolution fusion | flops 1612251136 | bytes 4456448 | tf_op jit(solution)/shard_map/uv,pmvw->pmuw/dot_general | solution.py:19
  127.5 4.7 %fusion.35 = f32[8,256,256]{2,1,0:T(8,128)S(1)} fusion(f32[8,256,256]{2,1,0:T(8,128)S(1)} %fusion.24, f32[8,256,256]{2,1,0:T(8,128)S(1)} %fusion.38, f32[256,256]{1,0:T(8,128)S(1)} %fusion.64), kind=kOutput, calls=%fused_computation.50 | convolution fusion | flops 1612775424 | bytes 6553600 | tf_op jit(solution)/shard_map/uv,pmvw->pmuw/dot_general | solution.py:22
  132.3 4.5 %fusion.8 = f32[8,256,256]{2,1,0:T(8,128)S(1)} fusion(f32[8,256,256]{2,1,0:T(8,128)S(1)} %fusion.35), kind=kOutput, calls=%fused_computation.22 | convolution fusion | flops 1611595776 | bytes 4194304 | tf_op jit(solution)/shard_map/pmuv,vw->pmuw/dot_general | solution.py:28
  136.8 4.5 %fusion.10 = f32[8,256,256]{2,1,0:T(8,128)S(1)} fusion(f32[8,256,256]{2,1,0:T(8,128)S(1)} %fusion.35), kind=kOutput, calls=%fused_computation.24 | convolution fusion | flops 1611726848 | bytes 4194304 | tf_op jit(solution)/shard_map/pmuv,vw->pmuw/dot_general | solution.py:25
  141.3 4.8 %fusion.32 = f32[8,256,256]{2,1,0:T(8,128)S(1)} fusion(f32[8,256,256]{2,1,0:T(8,128)S(1)} %fusion.26, f32[8,256,256]{2,1,0:T(8,128)S(1)} %fusion.38, f32[256,256]{1,0:T(8,128)S(1)} %fusion.64), kind=kOutput, calls=%fused_computation.49 | convolution fusion | flops 1612644352 | bytes 6553600 | tf_op jit(solution)/shard_map/uv,pmvw->pmuw/dot_general | solution.py:19
  150.5 5.6 %add_bitcast_fusion = (f32[8,1,256,256]{3,2,0,1:T(8,128)S(1)}, f32[8,1,256,256]{3,2,0,1:T(8,128)S(1)}, f32[256,256]{1,0:T(8,128)S(1)}, f32[256,256]{1,0:T(8,128)S(1)}, f32[256,256]{1,0:T(8,128)S(1)}) fusion(f32[8,256,256]{2,1,0:T(8,128)S(1)} %fusion.47, f32[256,256]{1,0:T(8,128)S(1)} %get-tuple-element.130, f32[256,256]{1,0:T(8,128)S(1)} %get-tuple-element.129, ...), kind=kOutput, calls=%fused_computation.39 | convolution fusion | flops 1621360640 | bytes 15990784 | tf_op jit(solution)/shard_map/pmuv,vw->pmuw/dot_general | solution.py:25
  163.1 4.6 %scatter.4 = f32[1,3,512,256]{3,2,1,0:T(8,128)S(1)} dynamic-update-slice(f32[1,3,512,256]{3,2,1,0:T(8,128)S(1)} %broadcast_in_dim.13, f32[1,3,256,256]{3,2,1,0:T(8,128)S(1)} %maximum_select_fusion, s32[]{:T(128)} %constant.126.clone.1, s32[]{:T(128)} %constant.126.clone.1, s32[]{:T(128)} %bitcast.46, s32[]{:T(128)} %constant.126.clone.1) | dynamic-update-slice | bytes 1572868 | tf_op jit(solution)/shard_map/vmap(vmap())/scatter | solution.py:94
  172.7 23.2 %all-to-all-done.1 = f32[1,3,4,128,256]{4,3,1,0,2:T(8,128)S(1)} async-done(((f32[1,3,4,128,256]{4,3,1,0,2:T(8,128)}), f32[1,3,4,128,256]{4,3,1,0,2:T(8,128)S(1)}, u32[]{:S(2)}, u32[]{:S(2)}) %all-to-all-start.1) | async-done | bytes 1572896 | tf_op jit(solution)/shard_map/all_to_all | solution.py:99
  197.6 34.7 %while.15 = (s32[]{:T(128)}, f32[3,128,2048]{2,1,0:T(8,128)S(1)}, s32[4,1,2]{0,2,1:T(2,128)S(1)}, f32[3,4,128,256]{3,2,0,1:T(8,128)}, s32[]{:T(128)}, /*index=5*/s32[]{:T(128)}, s32[]{:T(128)}) while((s32[]{:T(128)}, f32[3,128,2048]{2,1,0:T(8,128)S(1)}, s32[4,1,2]{0,2,1:T(2,128)S(1)}, f32[3,4,128,256]{3,2,0,1:T(8,128)}, s32[]{:T(128)}, ...), condition=%wide.region_6.7_spmd, body=%wide.region_5.6_spmd.sunk | while | flops 98309 | bytes 1966215 | solution.py:109
  201.0 4.7 %dynamic_update_slice.8 = f32[3,128,2048]{2,1,0:T(8,128)S(1)} dynamic-update-slice(f32[3,128,2048]{2,1,0:T(8,128)S(1)} %get-tuple-element.174, f32[3,128,256]{2,1,0:T(8,128)S(1)} %bitcast_add_fusion.2, s32[]{:T(128)} %constant.126.clone.1..sunk, s32[]{:T(128)} %constant.126.clone.1..sunk, s32[]{:T(128)S(6)} %select_n.164) | dynamic-update-slice | bytes 786436 | tf_op jit(solution)/shard_map/while/body/eval_jaxpr/dynamic_update_slice | solution.py:107
  209.1 5.5 %dynamic_update_slice.8 = f32[3,128,2048]{2,1,0:T(8,128)S(1)} dynamic-update-slice(f32[3,128,2048]{2,1,0:T(8,128)S(1)} %get-tuple-element.174, f32[3,128,256]{2,1,0:T(8,128)S(1)} %bitcast_add_fusion.2, s32[]{:T(128)} %constant.126.clone.1..sunk, s32[]{:T(128)} %constant.126.clone.1..sunk, s32[]{:T(128)S(6)} %select_n.164) | dynamic-update-slice | bytes 786436 | tf_op jit(solution)/shard_map/while/body/eval_jaxpr/dynamic_update_slice | solution.py:107
  217.9 5.5 %dynamic_update_slice.8 = f32[3,128,2048]{2,1,0:T(8,128)S(1)} dynamic-update-slice(f32[3,128,2048]{2,1,0:T(8,128)S(1)} %get-tuple-element.174, f32[3,128,256]{2,1,0:T(8,128)S(1)} %bitcast_add_fusion.2, s32[]{:T(128)} %constant.126.clone.1..sunk, s32[]{:T(128)} %constant.126.clone.1..sunk, s32[]{:T(128)S(6)} %select_n.164) | dynamic-update-slice | bytes 786436 | tf_op jit(solution)/shard_map/while/body/eval_jaxpr/dynamic_update_slice | solution.py:107
  226.8 5.5 %dynamic_update_slice.8 = f32[3,128,2048]{2,1,0:T(8,128)S(1)} dynamic-update-slice(f32[3,128,2048]{2,1,0:T(8,128)S(1)} %get-tuple-element.174, f32[3,128,256]{2,1,0:T(8,128)S(1)} %bitcast_add_fusion.2, s32[]{:T(128)} %constant.126.clone.1..sunk, s32[]{:T(128)} %constant.126.clone.1..sunk, s32[]{:T(128)S(6)} %select_n.164) | dynamic-update-slice | bytes 786436 | tf_op jit(solution)/shard_map/while/body/eval_jaxpr/dynamic_update_slice | solution.py:107
  234.1 37.6 %all-reduce.4.cloned.1.call-done = (f32[8,2,256,256]{3,2,0,1:T(8,128)}, f32[256,256]{1,0:T(8,128)}) async-done(((f32[8,2,256,256]{3,2,0,1:T(8,128)}, f32[256,256]{1,0:T(8,128)}), (f32[8,2,256,256]{3,2,0,1:T(8,128)}, f32[256,256]{1,0:T(8,128)})) %all-reduce.4.cloned.1.call-update) | async-done | bytes 4456464 | tf_op jit(solution)/shard_map/psum | solution.py:121
  275.0 59.4 %reduce-scatter.2.cloned.1.call-done = f32[3,128,512]{2,1,0:T(8,128)} async-done(((f32[3,128,2048]{2,1,0:T(8,128)}), f32[3,128,512]{2,1,0:T(8,128)}) %reduce-scatter.2.cloned.1.call-update) | async-done | bytes 786448 | tf_op jit(solution)/shard_map/reduce_scatter | solution.py:110
  (58 shorter events, 56.1 us)
Async XLA Ops:
  7.2 48.2 %all-gather.2.cloned.1.call-start = ((), (), s32[]{:S(2)}) async-start(), calls=%async_computation.3 | async-start | bytes 2621440 | tf_op jit(solution)/shard_map/all_gather | solution.py:53
  60.1 18.0 %all-to-all-start = ((f32[1,2,4,128,256]{3,1,4,0,2:T(2,128)}), f32[1,2,4,128,256]{3,1,4,0,2:T(2,128)S(1)}, u32[]{:S(2)}, u32[]{:S(2)}) async-start(f32[1,2,4,128,256]{3,1,4,0,2:T(2,128)} %fusion.50), calls=%async_computation | async-start | bytes 2097152 | tf_op jit(solution)/shard_map/all_to_all | solution.py:67
  64.5 207.1 %all-reduce.4.cloned.1.call-start = ((), (), s32[]{:S(2)}) async-start(), calls=%async_computation.5 | async-start | bytes 8912896 | tf_op jit(solution)/shard_map/psum | solution.py:121
  79.6 6.9 %copy-start = (f32[8,2,256,256]{3,2,1,0:T(8,128)S(1)}, f32[8,2,256,256]{3,2,1,0:T(8,128)}, u32[]{:S(2)}) copy-start(f32[8,2,256,256]{3,2,1,0:T(8,128)} %param.9) | copy-start | bytes 12582916
  113.9 4.6 %copy-start.3 = (f32[1,256,256]{2,1,0:T(8,128)S(1)}, f32[1,256,256]{2,1,0:T(8,128)}, u32[]{:S(2)}) copy-start(f32[1,256,256]{2,1,0:T(8,128)} %param.10) | copy-start | bytes 786436
  158.4 0.7 copy-start.5
  158.4 1.3 copy-start.4
  169.1 26.9 %all-to-all-start.1 = ((f32[1,3,4,128,256]{4,3,1,0,2:T(8,128)}), f32[1,3,4,128,256]{4,3,1,0,2:T(8,128)S(1)}, u32[]{:S(2)}, u32[]{:S(2)}) async-start(f32[1,3,4,128,256]{4,3,1,0,2:T(8,128)} %copy.72), calls=%async_computation.1 | async-start | bytes 3145728 | tf_op jit(solution)/shard_map/all_to_all | solution.py:99
  172.7 161.7 %reduce-scatter.2.cloned.1.call-start = ((), (), s32[]{:S(2)}) async-start(), calls=%async_computation.4 | async-start | bytes 3932160 | tf_op jit(solution)/shard_map/reduce_scatter | solution.py:110
  196.0 1.2 copy-start.2
  232.3 1.8 copy-start.1
Sparse Core Ops, SparseCore 0:
  10.1 45.1 all-gather.1
  158.6 113.0 all-reduce.3
  274.0 60.4 reduce-scatter.1
where the time goes:
time: 349 us; the launch traced here: 344 us
  waiting for transfers between devices  178 us (51%)
  matrix products  76.3 us (22%)
  local copies, waits for them, and re-layouts  42.3 us (12%)
  other arithmetic  18.1 us (5%)
  between operations  14.3 us (4%)
  starting transfers between devices  8.1 us (2%)
  loops' own time  6.7 us (2%)
    reduce_scatter x1, waiting for transfers between devices, body(): lax.psum_scatter(strip_grad, 'tile', scatter_dimension=2, tiled=True)  59.4 us
    all_gather x1, waiting for transfers between devices, body(): strip = lax.all_gather(object_field, 'tile', axis=2, tiled=True)  44.7 us
    psum x1, waiting for transfers between devices, body(): lax.psum((probe_numer, probe_weight), ('scan', 'tile'))  37.6 us
    all_to_all x1, waiting for transfers between devices, body(): lax.all_to_all(placed, 'scan', split_axis=2, concat_axis=2, tiled=True)  23.2 us
    dynamic_update_slice x4, local copies, waits for them, and re-layouts, add_piece(): lax.dynamic_update_slice(strip_acc, window + block_piece, (anchor, anchor...  21.1 us
    all_to_all x1, waiting for transfers between devices, body(): lax.all_to_all(outgoing, 'scan', split_axis=2, concat_axis=2, tiled=True)  13.3 us
    dot_general x2, matrix products, transform(): jnp.einsum('uv,pmvw->pmuw', cos_table, real_part, precision=highest)  11.7 us
    dot_general x2, matrix products, transform(): jnp.einsum('pmuv,vw->pmuw', left_re, cos_table, precision=highest)  10 us
  transfers between devices with their start and end apart: 5, of which 5 were waited for; matrix products, arithmetic and copies ran while one was open for 13% of the time, Pallas kernels for 0%

commit v1 on v0

v1 whole, which is shorter than its diff:
```python
import functools
import math

import jax
import jax.numpy as jnp
import numpy as np
from jax import lax
from jax.experimental import pallas as pl
from jax.experimental.pallas import tpu as pltpu
from jax.sharding import PartitionSpec as P

F32 = jnp.float32
BF16 = jnp.bfloat16


def dft_blocks(length):
    steps = np.arange(length)
    angle = (steps[:, None] * steps[None, :] % length) * (2.0 * math.pi / length)
    factor = 1.0 / math.sqrt(length)
    cos = np.cos(angle) * factor
    sin = -np.sin(angle) * factor
    fwd = np.block([[cos, sin], [-sin, cos]]).astype(np.float32)
    inv = np.block([[cos, -sin], [sin, cos]]).astype(np.float32)
    tables = []
    for table in (fwd, inv):
        high = table.astype(jnp.bfloat16)
        low = (table - high.astype(np.float32)).astype(jnp.bfloat16)
        tables += [high, low]
    return np.stack(tables)


def split(x):
    high = x.astype(BF16)
    return high, (x - high.astype(F32)).astype(BF16)


def dot(a, b):
    return jnp.dot(a, b, preferred_element_type=F32)


def wave_kernel(edge, modes, patch, probe, measured, tables, numer, probe_numer, far, model):
    fwd_h, fwd_l, inv_h, inv_l = 0, 1, 2, 3

    def right(x, high_at, low_at):
        high, low = split(x)
        return dot(high, tables[high_at]) + dot(high, tables[low_at]) + dot(low, tables[high_at])

    def left(x, high_at, low_at):
        high, low = split(x)
        return dot(tables[high_at], high) + dot(tables[low_at], high) + dot(tables[high_at], low)

    def rows(x):
        return jnp.concatenate([x[:, :edge], x[:, edge:]], axis=0)

    model[...] = jnp.zeros_like(model)
    numer[...] = jnp.zeros_like(numer)

    def forward(k, carry):
        pr, pi = probe[k, 0], probe[k, 1]
        qr, qi = patch[0], patch[1]
        wave = jnp.concatenate([pr * qr - pi * qi, pr * qi + pi * qr], axis=1)
        out = left(rows(right(wave, fwd_h, fwd_l)), inv_h, inv_l)
        fr, fi = out[:edge], out[edge:]
        far[k, 0] = fr
        far[k, 1] = fi
        model[...] += fr * fr + fi * fi
        return carry

    lax.fori_loop(0, modes, forward, 0)
    model[...] = 2.0 * (model[...] - measured[...])

    def backward(k, carry):
        weight = model[...]
        wave = jnp.concatenate([weight * far[k, 0], weight * far[k, 1]], axis=1)
        out = left(rows(right(wave, inv_h, inv_l)), fwd_h, fwd_l)
        br, bi = out[:edge], out[edge:]
        pr, pi = probe[k, 0], probe[k, 1]
        qr, qi = patch[0], patch[1]
        numer[0] += pr * br + pi * bi
        numer[1] += pr * bi - pi * br
        probe_numer[k, 0] = qr * br + qi * bi
        probe_numer[k, 1] = qr * bi - qi * br
        return carry

    lax.fori_loop(0, modes, backward, 0)


def wave(patch, probe, measured):
    modes, _, edge, _ = probe.shape
    vmem = pl.BlockSpec(memory_space=pltpu.VMEM)
    return pl.pallas_call(
        functools.partial(wave_kernel, edge, modes),
        out_shape=(
            jax.ShapeDtypeStruct((2, edge, edge), F32),
            jax.ShapeDtypeStruct((modes, 2, edge, edge), F32),
        ),
        in_specs=[vmem] * 4,
        out_specs=(vmem, vmem),
        scratch_shapes=[pltpu.VMEM((modes, 2, edge, edge), F32), pltpu.VMEM((edge, edge), F32)],
        compiler_params=pltpu.CompilerParams(vmem_limit_bytes=40 * 2**20),
        cost_estimate=pl.CostEstimate(
            flops=modes * 48 * edge**3 * 2, bytes_accessed=modes * 16 * edge**2, transcendentals=0
        ),
    )(patch, probe, measured, jnp.asarray(dft_blocks(edge)))


def placement(start, offset, size, edge):
    at = start[:, None, None] + lax.broadcasted_iota(jnp.int32, (1, edge, size), 1)
    here = offset + lax.broadcasted_iota(jnp.int32, (1, edge, size), 2)
    return (at == here).astype(BF16)


def split_outside(x):
    high = lax.reduce_precision(x, 8, 7)
    return jnp.stack([high, x - high]).astype(BF16)


def place_exact(images, row_hot, col_hot):
    both = split_outside(images)
    cols = jnp.einsum("hpcab,pbj->hpcaj", both, col_hot, preferred_element_type=F32)
    cols = cols[0] + cols[1]
    both = split_outside(cols)
    out = jnp.einsum("pai,hpcaj->hcij", row_hot, both, preferred_element_type=F32)
    return out[0] + out[1]


def body(object_field, probe, measured, positions):
    strip_rows = object_field.shape[1]
    tile_cols = object_field.shape[2]
    pattern_count = measured.shape[0]
    edge_len = measured.shape[1]
    mode_count = probe.shape[0]
    scan_count = lax.axis_size("scan")
    tile_count = lax.axis_size("tile")
    scan_index = lax.axis_index("scan")
    tile_index = lax.axis_index("tile")
    total_rows = strip_rows * scan_count
    anchor = jnp.zeros((), jnp.int32)
    grid_pos = positions.reshape(scan_count, tile_count, pattern_count, 2)
    column_pos = lax.dynamic_index_in_dim(grid_pos, tile_index, axis=1, keepdims=False)
    row_pos = lax.dynamic_index_in_dim(grid_pos, scan_index, axis=0, keepdims=False)
    row_pos = row_pos.reshape(tile_count, 2)
    own_pos = lax.dynamic_index_in_dim(column_pos, scan_index, axis=0, keepdims=False)
    strip = lax.all_gather(object_field, "tile", axis=2, tiled=True)
    strip_top = scan_index * strip_rows
    tile_left = tile_index * tile_cols

    power = jnp.sum(probe[:, 0] * probe[:, 0] + probe[:, 1] * probe[:, 1], axis=0)
    all_rows = placement(positions[:, 0], strip_top, strip_rows, edge_len)
    all_cols = placement(positions[:, 1], tile_left, tile_cols, edge_len)
    power_all = jnp.broadcast_to(power, (positions.shape[0], 1) + power.shape)
    denom = place_exact(power_all, all_rows, all_cols)[0]
    denom = jnp.maximum(denom, 1.0)

    def cut_slice(position):
        row_at = position[0]
        block_piece = lax.dynamic_slice(
            strip, (anchor, anchor, position[1]), (2, strip_rows, edge_len)
        )
        intersections = jnp.logical_and(
            strip_top < row_at + edge_len, strip_top + strip_rows > row_at
        )
        return jnp.where(intersections, block_piece, 0.0)

    outgoing = jax.vmap(jax.vmap(cut_slice), out_axes=2)(column_pos)
    incoming = lax.all_to_all(outgoing, "scan", split_axis=2, concat_axis=2, tiled=True)
    column = incoming.reshape(2, total_rows, edge_len)
    patch = lax.dynamic_slice(column, (anchor, own_pos[0, 0], anchor), (2, edge_len, edge_len))

    numer, probe_numer = wave(patch, probe, measured[0])
    weight = jnp.sum(patch * patch, axis=0)

    numers = lax.all_gather(numer, "tile", axis=0)
    row_hot = placement(row_pos[:, 0], 0, total_rows, edge_len)
    col_hot = placement(row_pos[:, 1], tile_left, tile_cols, edge_len)
    placed = place_exact(numers, row_hot, col_hot)
    summed = lax.psum_scatter(placed, "scan", scatter_dimension=1, tiled=True)
    object_gradient = summed / denom[None]

    own = lax.psum_scatter(probe_numer, "tile", scatter_dimension=0, tiled=True)
    own = lax.psum(own, "scan")
    weight_all = lax.psum(weight, ("scan", "tile"))
    probe_gradient = own / (weight_all + 1e-05)[None, None]
    return (object_gradient, probe_gradient)


def solution(mesh):
    return jax.shard_map(
        body,
        mesh=mesh,
        in_specs=(
            P(None, ("groups", "scan"), "tile"),
            P("groups", None, None, None),
            P(("groups", "scan", "tile"), None, None),
            P("groups", None),
        ),
        out_specs=(P(None, ("groups", "scan"), "tile"), P(("groups", "tile"), None, None, None)),
        check_vma=False,
    )
```

time: 349 us -> 406 us (1.16)
  waiting for transfers between devices: 178 us -> 320 us
  matrix products: 76.3 us -> 10.2 us
  local copies, waits for them, and re-layouts: 42.3 us -> 15.3 us
  Pallas kernels: 0 us -> 19.5 us
  loops' own time: 6.7 us -> 0 us
    psum x1 -> x2, waiting for transfers between devices: 37.6 us -> 128 us  [the longest x1 92.3 us: body(): weight_all = lax.psum(weight, ('scan', 'tile'))]
    dot_general x16 -> x4, matrix products: 76.3 us -> 10.2 us  [the longest x2 5.27 us: place_exact(): jnp.einsum('hpcab,pbj->hpcaj', both, col_hot, preferred_element_type=F32)]
    all_gather x0 -> x1, waiting for transfers between devices: none -> 42.5 us  [body(): numers = lax.all_gather(numer, 'tile', axis=0)]
    reduce_scatter x1 -> x2, waiting for transfers between devices: 59.4 us -> 90.2 us  [the longest x1 56.1 us: body(): own = lax.psum_scatter(probe_numer, 'tile', scatter_dimension=0, tiled=True)]
    all_to_all x1 -> x0, waiting for transfers between devices: 23.2 us -> none  [body(): lax.all_to_all(placed, 'scan', split_axis=2, concat_axis=2, tiled=True)]
    dynamic_update_slice x4 -> x0, local copies, waits for them, and re-layouts: 21.1 us -> none  [add_piece(): lax.dynamic_update_slice(strip_acc, window + block_piece, (anchor, anchor...]
    pallas_call x0 -> x1, Pallas kernels: none -> 19.5 us  [wave(): pl.pallas_call(functools.partial(wave_kernel, edge, modes), out_shape=(ja...]
    another operation x1 -> x0, loops' own time: 6.7 us -> none  [body(): strip_grad = lax.fori_loop(0, scan_count, add_piece, strip_grad)]
  transfers between devices with their start and end apart: 5 -> 7, of which waited for: 5 -> 7; matrix products, arithmetic and copies ran while one was open for 13% -> 7% of each run, Pallas kernels for 0% -> 0%
where the time goes in v1:
time: 406 us; the launch traced here: 403 us
  waiting for transfers between devices  320 us (79%)
  Pallas kernels  19.5 us (5%)
  other arithmetic  18.7 us (5%)
  local copies, waits for them, and re-layouts  15.3 us (4%)
  between operations  14.4 us (4%)
  matrix products  10.2 us (3%)
  starting transfers between devices  4.8 us (1%)
    psum x1, waiting for transfers between devices, body(): weight_all = lax.psum(weight, ('scan', 'tile'))  92.3 us
    reduce_scatter x1, waiting for transfers between devices, body(): own = lax.psum_scatter(probe_numer, 'tile', scatter_dimension=0, tiled=True)  56.1 us
    all_gather x1, waiting for transfers between devices, body(): strip = lax.all_gather(object_field, 'tile', axis=2, tiled=True)  44.7 us
    all_gather x1, waiting for transfers between devices, body(): numers = lax.all_gather(numer, 'tile', axis=0)  42.5 us
    psum x1, waiting for transfers between devices, body(): own = lax.psum(own, 'scan')  35.8 us
    reduce_scatter x1, waiting for transfers between devices, body(): summed = lax.psum_scatter(placed, 'scan', scatter_dimension=1, tiled=True)  34.1 us
    pallas_call x1, Pallas kernels, wave(): pl.pallas_call(functools.partial(wave_kernel, edge, modes), out_shape=(ja...  19.5 us
    all_to_all x1, waiting for transfers between devices, body(): lax.all_to_all(outgoing, 'scan', split_axis=2, concat_axis=2, tiled=True)  13.3 us
  transfers between devices with their start and end apart: 7, of which 7 were waited for; matrix products, arithmetic and copies ran while one was open for 7% of the time, Pallas kernels for 0%

profile of v1, /device:TPU:13, one launch (start us, length us, event | category | flops | bytes accessed | tf_op | source)
XLA Modules:
  0.0 402.9 jit_solution(15961771003657074436)
XLA Ops:
  7.2 2.0 copy.23
  10.6 44.7 %all-gather.4.cloned.1.call-done = f32[2,128,2048]{1,0,2:T(2,128)} async-done(((f32[2,128,512]{1,0,2:T(2,128)}), f32[2,128,2048]{1,0,2:T(2,128)}) %all-gather.4.cloned.1.call-update) | async-done | bytes 2097168 | tf_op jit(solution)/shard_map/all_gather | solution.py:144
  55.4 3.3 gather_fusion
  58.7 1.5 fusion.38
  60.2 4.4 %all-to-all-start = ((f32[1,2,4,128,256]{3,1,4,0,2:T(2,128)}), f32[1,2,4,128,256]{3,1,4,0,2:T(2,128)S(1)}, u32[]{:S(2)}, u32[]{:S(2)}) async-start(f32[1,2,4,128,256]{3,1,4,0,2:T(2,128)} %fusion.38), calls=%async_computation | async-start | bytes 2097152 | tf_op jit(solution)/shard_map/all_to_all | solution.py:166
  64.9 13.3 %all-to-all-done = f32[1,2,4,128,256]{3,1,4,0,2:T(2,128)S(1)} async-done(((f32[1,2,4,128,256]{3,1,4,0,2:T(2,128)}), f32[1,2,4,128,256]{3,1,4,0,2:T(2,128)S(1)}, u32[]{:S(2)}, u32[]{:S(2)}) %all-to-all-start) | async-done | bytes 1048608 | tf_op jit(solution)/shard_map/all_to_all | solution.py:166
  79.5 1.8 multiply_reduce_fusion
  81.3 2.2 copy-done
  83.5 19.5 %shard_map.68 = (f32[2,256,256]{2,1,0:T(8,128)}, f32[8,2,256,256]{3,2,1,0:T(8,128)S(1)}) custom-call(f32[2,256,256]{2,1,0:T(8,128)S(1)} %get-tuple-element.13.patch, f32[8,2,256,256]{3,2,1,0:T(8,128)S(1)} %copy-done, f32[256,256]{1,0:T(8,128)S(1)} %bitcast.97, bf16[4,512,512]{2,1,0:T(8,128)(2,1)S(1)} %copy-done.3), custom_call_target="tpu_custom_call" | custom-call | flops 12884901888 | bytes 8388608 | tf_op jit(solution)/shard_map/pallas_call | solution.py:91
  103.0 1.9 copy-done.1
  106.3 42.5 %all-gather.6.cloned.1.call-done = f32[8,256,256]{2,1,0:T(8,128)} async-done(((f32[2,256,256]{2,1,0:T(8,128)}), f32[8,256,256]{2,1,0:T(8,128)}) %all-gather.6.cloned.1.call-update) | async-done | bytes 2097168 | tf_op jit(solution)/shard_map/all_gather | solution.py:173
  148.8 2.0 fusion.37
  152.9 2.5 fusion.11
  155.9 1.8 fusion.21
  158.0 3.0 add_reduce_fusion
  161.3 1.6 stack.41
  162.8 4.0 convolution_bitcast_fusion
  168.0 1.9 fusion.10
  169.9 2.4 fusion.31
  172.4 56.1 %reduce-scatter.5.cloned.1.call-done = f32[2,2,256,256]{3,2,1,0:T(8,128)} async-done(((f32[8,2,256,256]{3,2,1,0:T(8,128)}), f32[2,2,256,256]{3,2,1,0:T(8,128)}) %reduce-scatter.5.cloned.1.call-update) | async-done | bytes 1048592 | tf_op jit(solution)/shard_map/reduce_scatter | solution.py:180
  228.6 92.3 %all-reduce.6.cloned.1.call-done = f32[256,256]{1,0:T(8,128)} async-done(((f32[256,256]{1,0:T(8,128)}), f32[256,256]{1,0:T(8,128)}) %all-reduce.6.cloned.1.call-update) | async-done | bytes 262160 | tf_op jit(solution)/shard_map/psum | solution.py:182
  321.9 34.1 %reduce-scatter.3.cloned.1.call-done = f32[2,128,512]{1,2,0:T(8,128)} async-done(((f32[2,512,512]{1,2,0:T(8,128)}), f32[2,128,512]{1,2,0:T(8,128)}) %reduce-scatter.3.cloned.1.call-update) | async-done | bytes 524304 | tf_op jit(solution)/shard_map/reduce_scatter | solution.py:177
  358.0 35.8 %all-reduce.4.cloned.1.call-done = f32[2,2,256,256]{3,2,1,0:T(8,128)} async-done(((f32[2,2,256,256]{3,2,1,0:T(8,128)}), f32[2,2,256,256]{3,2,1,0:T(8,128)}) %all-reduce.4.cloned.1.call-update) | async-done | bytes 1048592 | tf_op jit(solution)/shard_map/psum | solution.py:181
  393.8 2.3 broadcast_divide_fusion
  (44 shorter events, 11.6 us)
Async XLA Ops:
  7.2 48.2 %all-gather.4.cloned.1.call-start = ((), (), s32[]{:S(2)}) async-start(), calls=%async_computation.3 | async-start | bytes 2621440 | tf_op jit(solution)/shard_map/all_gather | solution.py:144
  58.6 22.7 %copy-start.2 = (f32[1,256,256]{2,1,0:T(8,128)S(1)}, f32[1,256,256]{2,1,0:T(8,128)}, u32[]{:S(2)}) copy-start(f32[1,256,256]{2,1,0:T(8,128)} %param.7) | copy-start | bytes 786436
  58.6 22.7 %copy-start.3 = (bf16[4,512,512]{2,1,0:T(8,128)(2,1)S(1)}, bf16[4,512,512]{2,1,0:T(8,128)(2,1)}, u32[]{:S(2)}) copy-start(bf16[4,512,512]{2,1,0:T(8,128)(2,1)} %constant.61.clone.tables) | copy-start | bytes 6291460
  60.2 18.0 %all-to-all-start = ((f32[1,2,4,128,256]{3,1,4,0,2:T(2,128)}), f32[1,2,4,128,256]{3,1,4,0,2:T(2,128)S(1)}, u32[]{:S(2)}, u32[]{:S(2)}) async-start(f32[1,2,4,128,256]{3,1,4,0,2:T(2,128)} %fusion.38), calls=%async_computation | async-start | bytes 2097152 | tf_op jit(solution)/shard_map/all_to_all | solution.py:166
  64.6 84.2 %all-gather.6.cloned.1.call-start = ((), (), s32[]{:S(2)}) async-start(), calls=%async_computation.8 | async-start | bytes 2621440 | tf_op jit(solution)/shard_map/all_gather | solution.py:173
  81.3 2.2 copy-start
  103.0 1.9 copy-start.1
  104.9 123.6 %reduce-scatter.5.cloned.1.call-start = ((), (), s32[]{:S(2)}) async-start(), calls=%async_computation.5 | async-start | bytes 5242880 | tf_op jit(solution)/shard_map/reduce_scatter | solution.py:180
  105.7 215.2 %all-reduce.6.cloned.1.call-start = ((), (), s32[]{:S(2)}) async-start(), calls=%async_computation.7 | async-start | bytes 524288 | tf_op jit(solution)/shard_map/psum | solution.py:182
  106.2 249.7 %reduce-scatter.3.cloned.1.call-start = ((), (), s32[]{:S(2)}) async-start(), calls=%async_computation.4 | async-start | bytes 2621440 | tf_op jit(solution)/shard_map/reduce_scatter | solution.py:177
  155.9 2.1 copy-start.4
  157.7 236.0 %all-reduce.4.cloned.1.call-start = ((), (), s32[]{:S(2)}) async-start(), calls=%async_computation.6 | async-start | bytes 2097152 | tf_op jit(solution)/shard_map/psum | solution.py:181
Sparse Core Ops, SparseCore 0:
  10.1 45.1 all-gather.3
  105.1 43.6 all-gather.5
  151.1 77.3 reduce-scatter.4
  232.1 88.7 all-reduce.5
  323.4 32.4 reduce-scatter.2
  358.1 35.5 all-reduce.3

commit v2 on v1

--- a/solution.py
+++ b/solution.py
@@ -102,6 +102,168 @@
             flops=modes * 48 * edge**3 * 2, bytes_accessed=modes * 16 * edge**2, transcendentals=0
         ),
     )(patch, probe, measured, jnp.asarray(dft_blocks(edge)))
+
+
+MESH = pl.DeviceIdType.MESH
+
+
+def greet(counts):
+    barrier = pltpu.get_barrier_semaphore()
+    total = 0
+    for axis, count in counts:
+        me = lax.axis_index(axis)
+        for i in range(1, count):
+            pl.semaphore_signal(
+                barrier, inc=1, device_id={axis: lax.rem(me + i, count)}, device_id_type=MESH
+            )
+            total += 1
+    pl.semaphore_wait(barrier, total)
+
+
+def push(src, dst, sems, at, axis, peer):
+    copy = pltpu.make_async_remote_copy(
+        src_ref=src,
+        dst_ref=dst,
+        send_sem=sems.at[0, at],
+        recv_sem=sems.at[1, at],
+        device_id={axis: peer},
+        device_id_type=MESH,
+    )
+    copy.start()
+    return copy
+
+
+def first_kernel(
+    ns, nt, modes, part_rows, numer, probe_numer, weight, numers, part, weight_part, got, got_w, z_sems, p_sems, w_sems
+):
+    scan, tile = lax.axis_index("scan"), lax.axis_index("tile")
+    greet((("scan", ns), ("tile", nt)))
+    copies = []
+    for i in range(1, nt):
+        peer = lax.rem(tile + i, nt)
+        copies.append(push(numer, numers.at[i], z_sems, i - 1, "tile", peer))
+    sums = []
+    for i in range(1, ns):
+        peer = lax.rem(scan + i, ns)
+        span = pl.ds(pl.multiple_of(peer * part_rows, part_rows), part_rows)
+        sums.append(push(weight.at[span, :], got_w.at[i - 1], w_sems, i - 1, "scan", peer))
+        sums.append(push(probe_numer.at[:, :, span, :], got.at[i - 1], p_sems, i - 1, "scan", peer))
+    numers[0] = numer[...]
+    for copy in sums:
+        copy.wait()
+    mine = pl.ds(pl.multiple_of(scan * part_rows, part_rows), part_rows)
+    total = weight[mine, :]
+    for i in range(ns - 1):
+        total += got_w[i]
+    weight_part[...] = total
+
+    def add(k, carry):
+        value = probe_numer[k, :, mine, :]
+        for i in range(ns - 1):
+            value += got[i, k]
+        part[k] = value
+        return carry
+
+    lax.fori_loop(0, modes, add, 0)
+    for copy in copies:
+        copy.wait()
+
+
+def first(ns, nt, numer, probe_numer, weight):
+    modes, _, edge, _ = probe_numer.shape
+    part_rows = edge // ns
+    vmem = pl.BlockSpec(memory_space=pltpu.VMEM)
+    dma = pltpu.SemaphoreType.DMA
+    return pl.pallas_call(
+        functools.partial(first_kernel, ns, nt, modes, part_rows),
+        out_shape=(
+            jax.ShapeDtypeStruct((nt, 2, edge, edge), F32),
+            jax.ShapeDtypeStruct((modes, 2, part_rows, edge), F32),
+            jax.ShapeDtypeStruct((part_rows, edge), F32),
+        ),
+        in_specs=[vmem] * 3,
+        out_specs=(vmem,) * 3,
+        scratch_shapes=[
+            pltpu.VMEM((ns - 1, modes, 2, part_rows, edge), F32),
+            pltpu.VMEM((ns - 1, part_rows, edge), F32),
+            dma((2, nt - 1)),
+            dma((2, ns - 1)),
+            dma((2, ns - 1)),
+        ],
+        compiler_params=pltpu.CompilerParams(
+            collective_id=0, has_side_effects=True, vmem_limit_bytes=40 * 2**20
+        ),
+    )(numer, probe_numer, weight)
+
+
+def second_kernel(
+    ns, nt, own_modes, part_rows, placed, denom, part, weight_part, grad, probe_grad, got_o, got_p, got_w, o_sems, p_sems, w_sems, g_sems
+):
+    scan, tile = lax.axis_index("scan"), lax.axis_index("tile")
+    greet((("scan", ns), ("tile", nt)))
+    probe_copies, object_copies, last = [], [], []
+    for i in range(1, nt):
+        peer = lax.rem(tile + i, nt)
+        span = pl.ds(peer * own_modes, own_modes)
+        probe_copies.append(push(weight_part, got_w.at[i - 1], w_sems, i - 1, "tile", peer))
+        probe_copies.append(push(part.at[span], got_p.at[i - 1], p_sems, i - 1, "tile", peer))
+    for i in range(1, ns):
+        peer = lax.rem(scan + i, ns)
+        object_copies.append(push(placed.at[peer], got_o.at[i - 1], o_sems, i - 1, "scan", peer))
+    for copy in probe_copies:
+        copy.wait()
+    total = weight_part[...]
+    for i in range(nt - 1):
+        total += got_w[i]
+    scale = 1.0 / (total + 1e-05)
+    mine = pl.ds(pl.multiple_of(scan * part_rows, part_rows), part_rows)
+    for k in range(own_modes):
+        value = part[tile * own_modes + k]
+        for i in range(nt - 1):
+            value += got_p[i, k]
+        probe_grad[k, :, mine, :] = value * scale[None]
+    for i in range(1, ns):
+        peer = lax.rem(scan + i, ns)
+        rows = probe_grad.at[:, :, mine, :]
+        last.append(push(rows, rows, g_sems, i - 1, "scan", peer))
+    for copy in object_copies:
+        copy.wait()
+    for c in range(2):
+        value = placed[scan, c]
+        for i in range(ns - 1):
+            value += got_o[i, c]
+        grad[c] = value / denom[...]
+    for copy in last:
+        copy.wait()
+
+
+def second(ns, nt, placed, denom, part, weight_part):
+    modes, _, part_rows, edge = part.shape
+    own_modes = modes // nt
+    block = placed.shape[1:]
+    vmem = pl.BlockSpec(memory_space=pltpu.VMEM)
+    dma = pltpu.SemaphoreType.DMA
+    return pl.pallas_call(
+        functools.partial(second_kernel, ns, nt, own_modes, part_rows),
+        out_shape=(
+            jax.ShapeDtypeStruct(block, F32),
+            jax.ShapeDtypeStruct((own_modes, 2, edge, edge), F32),
+        ),
+        in_specs=[vmem] * 4,
+        out_specs=(vmem,) * 2,
+        scratch_shapes=[
+            pltpu.VMEM((ns - 1,) + block, F32),
+            pltpu.VMEM((nt - 1, own_modes, 2, part_rows, edge), F32),
+            pltpu.VMEM((nt - 1, part_rows, edge), F32),
+            dma((2, ns - 1)),
+            dma((2, nt - 1)),
+            dma((2, nt - 1)),
+            dma((2, ns - 1)),
+        ],
+        compiler_params=pltpu.CompilerParams(
+            collective_id=1, has_side_effects=True, vmem_limit_bytes=40 * 2**20
+        ),
+    )(placed, denom, part, weight_part)
 
 
 def placement(start, offset, size, edge):
@@ -170,17 +332,16 @@
     numer, probe_numer = wave(patch, probe, measured[0])
     weight = jnp.sum(patch * patch, axis=0)
 
-    numers = lax.all_gather(numer, "tile", axis=0)
+    numers, part, weight_part = first(scan_count, tile_count, numer, probe_numer, weight)
+    sources = lax.rem(tile_index + tile_count - lax.iota(jnp.int32, tile_count), tile_count)
+    row_pos = row_pos[sources]
     row_hot = placement(row_pos[:, 0], 0, total_rows, edge_len)
     col_hot = placement(row_pos[:, 1], tile_left, tile_cols, edge_len)
     placed = place_exact(numers, row_hot, col_hot)
-    summed = lax.psum_scatter(placed, "scan", scatter_dimension=1, tiled=True)
-    object_gradient = summed / denom[None]
-
-    own = lax.psum_scatter(probe_numer, "tile", scatter_dimension=0, tiled=True)
-    own = lax.psum(own, "scan")
-    weight_all = lax.psum(weight, ("scan", "tile"))
-    probe_gradient = own / (weight_all + 1e-05)[None, None]
+    placed = placed.reshape(2, scan_count, strip_rows, tile_cols).transpose(1, 0, 2, 3)
+    object_gradient, probe_gradient = second(
+        scan_count, tile_count, placed, denom, part, weight_part
+    )
     return (object_gradient, probe_gradient)
 
 

time: 406 us -> 215 us (0.53)
  waiting for transfers between devices: 320 us -> 35.2 us
  Pallas kernels: 19.5 us -> 115 us
  other arithmetic: 18.7 us -> 13.1 us
  matrix products: 10.2 us -> 14.6 us
    psum x2 -> x0, waiting for transfers between devices: 128 us -> none  [the longest x1 92.3 us: body(): weight_all = lax.psum(weight, ('scan', 'tile'))]
    pallas_call x0 -> x2, Pallas kernels: none -> 96.7 us  [the longest x1 51.4 us: first(): pl.pallas_call(functools.partial(first_kernel, ns, nt, modes, part_rows),...]
    reduce_scatter x2 -> x0, waiting for transfers between devices: 90.2 us -> none  [the longest x1 56.1 us: body(): own = lax.psum_scatter(probe_numer, 'tile', scatter_dimension=0, tiled=True)]
    all_gather x1 -> x0, waiting for transfers between devices: 42.5 us -> none  [body(): numers = lax.all_gather(numer, 'tile', axis=0)]
    all_gather x1, waiting for transfers between devices: 44.7 us -> 28.4 us  [body(): strip = lax.all_gather(object_field, 'tile', axis=2, tiled=True)]
    all_to_all x1, waiting for transfers between devices: 13.3 us -> 6.7 us  [body(): lax.all_to_all(outgoing, 'scan', split_axis=2, concat_axis=2, tiled=True)]
    dot_general x2, matrix products: 4.97 us -> 9.3 us  [place_exact(): jnp.einsum('pai,hpcaj->hcij', row_hot, both, preferred_element_type=F32)]
  transfers between devices with their start and end apart: 7 -> 2, of which waited for: 7 -> 2; matrix products, arithmetic and copies ran while one was open for 7% -> 11% of each run, Pallas kernels for 0% -> 0%
where the time goes in v2:
time: 215 us
  Pallas kernels  115 us (53%)
  waiting for transfers between devices  35.2 us (16%)
  local copies, waits for them, and re-layouts  16.8 us (8%)
  matrix products  14.6 us (7%)
  between operations  14.4 us (7%)
  other arithmetic  13.1 us (6%)
  starting transfers between devices  5.18 us (2%)
    pallas_call x1, Pallas kernels, first(): pl.pallas_call(functools.partial(first_kernel, ns, nt, modes, part_rows),...  51.4 us
    pallas_call x1, Pallas kernels, second(): pl.pallas_call(functools.partial(second_kernel, ns, nt, own_modes, part_r...  45.3 us
    all_gather x1, waiting for transfers between devices, body(): strip = lax.all_gather(object_field, 'tile', axis=2, tiled=True)  28.4 us
    pallas_call x1, Pallas kernels, wave(): pl.pallas_call(functools.partial(wave_kernel, edge, modes), out_shape=(ja...  18.7 us
    dot_general x2, matrix products, place_exact(): jnp.einsum('pai,hpcaj->hcij', row_hot, both, preferred_element_type=F32)  9.3 us
    all_to_all x1, waiting for transfers between devices, body(): lax.all_to_all(outgoing, 'scan', split_axis=2, concat_axis=2, tiled=True)  6.7 us
    another operation x3, other arithmetic, split_outside(): return jnp.stack([high, x - high]).astype(BF16)  6.14 us
    unnamed x10, local copies, waits for them, and re-layouts  6.09 us
  transfers between devices with their start and end apart: 2, of which 2 were waited for; matrix products, arithmetic and copies ran while one was open for 11% of the time, Pallas kernels for 0%

profile of v2, /device:TPU:13, one launch (start us, length us, event | category | flops | bytes accessed | tf_op | source)
XLA Modules:
  0.0 214.7 jit_solution(16444937090719617087)
XLA Ops:
  7.2 2.0 copy.27
  9.4 0.8 reshape.139
  12.7 2.6 %add_reduce_fusion = f32[256,256]{1,0:T(8,128)S(1)} fusion(f32[8,2,256,256]{3,2,1,0:T(8,128)} %probe.1), kind=kLoop, calls=%fused_computation.39 | loop fusion | flops 2031616 | bytes 4456448 | tf_op jit(solution)/shard_map/reduce_sum | solution.py:310
  15.6 1.6 stack.41
  17.1 4.0 %convolution_bitcast_fusion = f32[2,16,1,256,512]{3,4,0,1,2:T(8,128)S(1)} fusion(bf16[1,16,256,256]{3,2,0,1:T(8,128)(2,1)} %stack.41, bf16[1,16,256,256]{3,2,0,1:T(8,128)(2,1)S(1)} %stack.40, s32[512]{0:T(512)S(1)} %iota_add_fusion, s32[16]{0:T(128)S(1)} %get-tuple-element.23), kind=kOutput, calls=%fused_computation.2 | convolution fusion | flops 2160066560 | bytes 20973632 | tf_op jit(solution)/shard_map/hpcab,pbj->hpcaj/dot_general | solution.py:282
  21.2 2.6 %fusion.9 = bf16[1,16,256,512]{2,3,1,0:T(8,128)(2,1)} fusion(f32[2,16,1,256,512]{3,4,0,1,2:T(8,128)S(1)} %convolution_bitcast_fusion), kind=kLoop, calls=%fused_computation.17 | loop fusion | flops 6291456 | bytes 20971520 | tf_op jit(solution)/shard_map/stack | solution.py:277
  23.7 3.2 %fusion.10 = bf16[1,16,256,512]{2,3,1,0:T(8,128)(2,1)} fusion(f32[2,16,1,256,512]{3,4,0,1,2:T(8,128)S(1)} %convolution_bitcast_fusion), kind=kLoop, calls=%fused_computation.18 | loop fusion | flops 8388608 | bytes 20971520 | tf_op jit(solution)/shard_map/stack | solution.py:277
  26.9 28.4 %all-gather.2.cloned.1.call-done = f32[2,128,2048]{1,0,2:T(2,128)} async-done(((f32[2,128,512]{1,0,2:T(2,128)}), f32[2,128,2048]{1,0,2:T(2,128)}) %all-gather.2.cloned.1.call-update) | async-done | bytes 2097168 | tf_op jit(solution)/shard_map/all_gather | solution.py:306
  55.4 3.3 %gather_fusion.1 = f32[4,2,128,256]{2,1,3,0:T(2,128)S(1)} fusion(f32[2,128,2048]{1,0,2:T(2,128)} %all-gather.2.cloned.1.call-done, s32[4]{0:T(128)S(1)} %or_reduce_fusion), kind=kCustom, calls=%fused_computation.1 | custom fusion | bytes 2097200 | tf_op jit(solution)/shard_map/vmap(vmap())/gather | solution.py:319
  58.6 1.5 fusion.35
  60.1 5.1 %all-to-all-start = ((f32[1,2,4,128,256]{3,1,4,0,2:T(2,128)}), f32[1,2,4,128,256]{3,1,4,0,2:T(2,128)}, u32[]{:S(2)}, u32[]{:S(2)}) async-start(f32[1,2,4,128,256]{3,1,4,0,2:T(2,128)} %fusion.35), calls=%async_computation | async-start | bytes 2097152 | tf_op jit(solution)/shard_map/all_to_all | solution.py:328
  65.3 6.9 %fusion.28 = f32[2,1,128,512]{3,2,1,0:T(8,128)S(1)} fusion(bf16[1,16,256,512]{2,3,1,0:T(8,128)(2,1)} %fusion.10, bf16[1,16,256,512]{2,3,1,0:T(8,128)(2,1)} %fusion.9, s32[128]{0:T(128)S(1)} %iota_add_fusion.1, s32[16]{0:T(128)S(1)} %get-tuple-element.22), kind=kOutput, calls=%fused_computation.45 | convolution fusion | flops 1078984704 | bytes 8913472 | tf_op jit(solution)/shard_map/pai,hpcaj->hcij/dot_general | solution.py:285
  72.3 6.7 %all-to-all-done = f32[1,2,4,128,256]{3,1,4,0,2:T(2,128)} async-done(((f32[1,2,4,128,256]{3,1,4,0,2:T(2,128)}), f32[1,2,4,128,256]{3,1,4,0,2:T(2,128)}, u32[]{:S(2)}, u32[]{:S(2)}) %all-to-all-start) | async-done | bytes 1048608 | tf_op jit(solution)/shard_map/all_to_all | solution.py:328
  79.0 2.3 %copy.30 = f32[1,2,4,128,256]{4,3,2,1,0:T(8,128)} copy(f32[1,2,4,128,256]{3,1,4,0,2:T(2,128)} %all-to-all-done) | data formatting | bytes 2097152 | tf_op jit(solution)/shard_map/all_to_all | solution.py:328
  81.2 1.2 multiply_reduce_fusion
  82.4 2.2 %copy-done = f32[8,2,256,256]{3,2,1,0:T(8,128)S(1)} copy-done((f32[8,2,256,256]{3,2,1,0:T(8,128)S(1)}, f32[8,2,256,256]{3,2,1,0:T(8,128)}, u32[]{:S(2)}) %copy-start) | copy-done | bytes 4194328
  84.6 18.7 %shard_map.68 = (f32[2,256,256]{2,1,0:T(8,128)S(1)}, f32[8,2,256,256]{3,2,1,0:T(8,128)S(1)}) custom-call(f32[2,256,256]{2,1,0:T(8,128)S(1)} %get-tuple-element.15.patch, f32[8,2,256,256]{3,2,1,0:T(8,128)S(1)} %copy-done, f32[256,256]{1,0:T(8,128)S(1)} %bitcast.92, bf16[4,512,512]{2,1,0:T(8,128)(2,1)S(1)} %copy-done.2), custom_call_target="tpu_custom_call" | custom-call | flops 12884901888 | bytes 8388608 | tf_op jit(solution)/shard_map/pallas_call | solution.py:91
  103.3 51.4 %shard_map.69 = (f32[4,2,256,256]{3,2,1,0:T(8,128)S(1)}, f32[8,2,64,256]{3,2,1,0:T(8,128)S(1)}, f32[64,256]{1,0:T(8,128)S(1)}) custom-call(f32[2,256,256]{2,1,0:T(8,128)S(1)} %get-tuple-element.7.numer, f32[8,2,256,256]{3,2,1,0:T(8,128)S(1)} %get-tuple-element.8.probe_numer, f32[256,256]{1,0:T(8,128)S(1)} %get-tuple-element.14.weight), custom_call_target="tpu_custom_call" | custom-call | tf_op jit(solution)/shard_map/pallas_call | solution.py:177
  155.1 1.3 convolution_bitcast_fusion.1
  156.4 0.9 reduce-precision_convert_fusion
  157.3 2.4 %fusion.11 = f32[2,2,512,512,1]{2,3,1,0,4:T(8,128)S(1)} fusion(bf16[1,4,2,256,512]{3,4,2,0,1:T(8,128)(2,1)S(1)} %get-tuple-element.17, bf16[1,4,2,256,512]{3,4,2,0,1:T(8,128)(2,1)S(1)} %get-tuple-element.16, s32[4]{0:T(128)S(1)} %get-tuple-element.12), kind=kOutput, calls=%fused_computation.20 | convolution fusion | flops 2150629376 | bytes 8388624 | tf_op jit(solution)/shard_map/pai,hpcaj->hcij/dot_general | solution.py:285
  160.8 45.3 %shard_map.70 = (f32[2,128,512]{2,1,0:T(8,128)S(1)}, f32[2,2,256,256]{3,2,1,0:T(8,128)S(1)}) custom-call(f32[4,2,128,512]{3,2,1,0:T(8,128)S(1)} %bitcast.91, f32[128,512]{1,0:T(8,128)S(1)} %fusion.43.denom, f32[8,2,64,256]{3,2,1,0:T(8,128)S(1)} %get-tuple-element.10.part, f32[64,256]{1,0:T(8,128)S(1)} %get-tuple-element.11.weight_part), custom_call_target="tpu_custom_call" | custom-call | tf_op jit(solution)/shard_map/pallas_call | solution.py:246
  206.1 0.8 copy.53
  206.9 1.0 copy.54
  (30 shorter events, 4.3 us)
Async XLA Ops:
  7.2 48.2 %all-gather.2.cloned.1.call-start = ((), (), s32[]{:S(2)}) async-start(), calls=%async_computation.1 | async-start | bytes 2621440 | tf_op jit(solution)/shard_map/all_gather | solution.py:306
  60.1 18.8 %all-to-all-start = ((f32[1,2,4,128,256]{3,1,4,0,2:T(2,128)}), f32[1,2,4,128,256]{3,1,4,0,2:T(2,128)}, u32[]{:S(2)}, u32[]{:S(2)}) async-start(f32[1,2,4,128,256]{3,1,4,0,2:T(2,128)} %fusion.35), calls=%async_computation | async-start | bytes 2097152 | tf_op jit(solution)/shard_map/all_to_all | solution.py:328
  72.2 10.2 %copy-start.1 = (f32[1,256,256]{2,1,0:T(8,128)S(1)}, f32[1,256,256]{2,1,0:T(8,128)}, u32[]{:S(2)}) copy-start(f32[1,256,256]{2,1,0:T(8,128)} %param.7) | copy-start | bytes 786436
  72.2 10.2 %copy-start.2 = (bf16[4,512,512]{2,1,0:T(8,128)(2,1)S(1)}, bf16[4,512,512]{2,1,0:T(8,128)(2,1)}, u32[]{:S(2)}) copy-start(bf16[4,512,512]{2,1,0:T(8,128)(2,1)} %constant.64.clone.tables) | copy-start | bytes 6291460
  82.4 2.2 %copy-start = (f32[8,2,256,256]{3,2,1,0:T(8,128)S(1)}, f32[8,2,256,256]{3,2,1,0:T(8,128)}, u32[]{:S(2)}) copy-start(f32[8,2,256,256]{3,2,1,0:T(8,128)} %probe.1) | copy-start | bytes 12582916
Sparse Core Ops, SparseCore 0:
  10.1 45.1 all-gather.1

commit v3 on v2

--- a/solution.py
+++ b/solution.py
@@ -133,22 +133,166 @@
     return copy
 
 
+def relay(nt, slots, sems):
+    tile = lax.axis_index("tile")
+
+    def copy(slot, way, hop, peer):
+        at = jnp.clip(slot, 0, nt - 1)
+        return pltpu.make_async_remote_copy(
+            src_ref=slots.at[at],
+            dst_ref=slots.at[at],
+            send_sem=sems.at[0, way, hop],
+            recv_sem=sems.at[1, way, hop],
+            device_id={"tile": jnp.clip(peer, 0, nt - 1)},
+            device_id_type=MESH,
+        )
+
+    def sends(hop, act):
+        pl.when(jnp.logical_and(tile + 1 < nt, tile - hop >= 0))(
+            lambda: act(copy(tile - hop, 0, hop, tile + 1))
+        )
+        pl.when(jnp.logical_and(tile - 1 >= 0, tile + hop < nt))(
+            lambda: act(copy(tile + hop, 1, hop, tile - 1))
+        )
+
+    def start(hop):
+        sends(hop, lambda c: c.start())
+
+    def finish(hop):
+        sends(hop, lambda c: c.wait_send())
+
+    def receive(hop):
+        pl.when(tile - 1 - hop >= 0)(lambda: copy(tile - 1 - hop, 0, hop, tile - 1).wait_recv())
+        pl.when(tile + 1 + hop < nt)(lambda: copy(tile + 1 + hop, 1, hop, tile + 1).wait_recv())
+
+    return start, receive, finish
+
+
+def hot(shape, row_start, col_start):
+    rows = row_start + lax.broadcasted_iota(jnp.int32, shape, 0)
+    cols = col_start + lax.broadcasted_iota(jnp.int32, shape, 1)
+    return (rows == cols).astype(F32).astype(BF16)
+
+
+def cut_kernel(
+    ns, nt, positions, tile_ref, probe, patch, denom, tiles, pieces, got, power, t_sems, s_sems
+):
+    scan, tile = lax.axis_index("scan"), lax.axis_index("tile")
+    strip_rows, tile_cols = tile_ref.shape[1:]
+    edge = patch.shape[1]
+    modes = probe.shape[0]
+    greet((("scan", ns), ("tile", nt)))
+    tiles[tile] = tile_ref[...]
+    start, receive, finish = relay(nt, tiles, t_sems)
+    start(0)
+    pieces[...] = jnp.zeros_like(pieces)
+
+    def cut(slot):
+        high, low = split(tiles[slot].reshape(2 * strip_rows, tile_cols))
+
+        def one(i, carry):
+            col_at = positions[i * nt + tile, 1]
+            pick = hot((tile_cols, edge), slot * tile_cols, col_at)
+            pieces[i] += (dot(high, pick) + dot(low, pick)).reshape(2, strip_rows, edge)
+            return carry
+
+        lax.fori_loop(0, ns, one, 0)
+
+    cut(tile)
+    power[...] = jnp.zeros_like(power)
+
+    def add_power(k, carry):
+        power[...] += probe[k, 0] * probe[k, 0] + probe[k, 1] * probe[k, 1]
+        return carry
+
+    lax.fori_loop(0, modes, add_power, 0)
+    denom[...] = jnp.zeros_like(denom)
+
+    def add_weight(j, carry):
+        row_pick = hot((strip_rows, edge), scan * strip_rows, positions[j, 0])
+        col_pick = hot((edge, tile_cols), positions[j, 1], tile * tile_cols)
+        high, low = split(power[...])
+        rows = dot(row_pick, high) + dot(row_pick, low)
+        high, low = split(rows)
+        denom[...] += dot(high, col_pick) + dot(low, col_pick)
+        return carry
+
+    lax.fori_loop(0, positions.shape[0], add_weight, 0)
+    denom[...] = jnp.maximum(denom[...], 1.0)
+    for hop in range(nt - 1):
+        receive(hop)
+        if hop + 1 < nt - 1:
+            start(hop + 1)
+        pl.when(tile - 1 - hop >= 0)(lambda: cut(jnp.maximum(tile - 1 - hop, 0)))
+        pl.when(tile + 1 + hop < nt)(lambda: cut(jnp.minimum(tile + 1 + hop, nt - 1)))
+    copies = []
+    for i in range(1, ns):
+        peer = lax.rem(scan + i, ns)
+        copies.append(push(pieces.at[peer], got.at[i - 1], s_sems, i - 1, "scan", peer))
+    row_at = positions[scan * nt + tile, 0]
+
+    def add_rows(piece, source):
+        pick = hot((edge, strip_rows), row_at, source * strip_rows)
+        out = []
+        for c in range(2):
+            high, low = split(piece[c])
+            out.append(dot(pick, high) + dot(pick, low))
+        return jnp.stack(out)
+
+    patch[...] = add_rows(pieces[scan], scan)
+    for copy in copies:
+        copy.wait()
+    for i in range(1, ns):
+        patch[...] += add_rows(got[i - 1], lax.rem(scan + ns - i, ns))
+    for hop in range(nt - 1):
+        finish(hop)
+
+
+def cut(ns, nt, positions, tile_block, probe):
+    _, strip_rows, tile_cols = tile_block.shape
+    edge = probe.shape[2]
+    vmem = pl.BlockSpec(memory_space=pltpu.VMEM)
+    dma = pltpu.SemaphoreType.DMA
+    return pl.pallas_call(
+        functools.partial(cut_kernel, ns, nt),
+        out_shape=(
+            jax.ShapeDtypeStruct((2, edge, edge), F32),
+            jax.ShapeDtypeStruct((strip_rows, tile_cols), F32),
+        ),
+        in_specs=[pl.BlockSpec(memory_space=pltpu.SMEM), vmem, vmem],
+        out_specs=(vmem,) * 2,
+        scratch_shapes=[
+            pltpu.VMEM((nt, 2, strip_rows, tile_cols), F32),
+            pltpu.VMEM((ns, 2, strip_rows, edge), F32),
+            pltpu.VMEM((ns - 1, 2, strip_rows, edge), F32),
+            pltpu.VMEM((edge, edge), F32),
+            dma((2, 2, nt - 1)),
+            dma((2, ns - 1)),
+        ],
+        compiler_params=pltpu.CompilerParams(
+            collective_id=2, has_side_effects=True, vmem_limit_bytes=40 * 2**20
+        ),
+    )(positions, tile_block, probe)
+
+
 def first_kernel(
     ns, nt, modes, part_rows, numer, probe_numer, weight, numers, part, weight_part, got, got_w, z_sems, p_sems, w_sems
 ):
     scan, tile = lax.axis_index("scan"), lax.axis_index("tile")
     greet((("scan", ns), ("tile", nt)))
-    copies = []
-    for i in range(1, nt):
-        peer = lax.rem(tile + i, nt)
-        copies.append(push(numer, numers.at[i], z_sems, i - 1, "tile", peer))
+    numers[tile] = numer[...]
+    start, receive, finish = relay(nt, numers, z_sems)
+    start(0)
     sums = []
     for i in range(1, ns):
         peer = lax.rem(scan + i, ns)
         span = pl.ds(pl.multiple_of(peer * part_rows, part_rows), part_rows)
         sums.append(push(weight.at[span, :], got_w.at[i - 1], w_sems, i - 1, "scan", peer))
         sums.append(push(probe_numer.at[:, :, span, :], got.at[i - 1], p_sems, i - 1, "scan", peer))
-    numers[0] = numer[...]
+    for hop in range(nt - 1):
+        receive(hop)
+        if hop + 1 < nt - 1:
+            start(hop + 1)
     for copy in sums:
         copy.wait()
     mine = pl.ds(pl.multiple_of(scan * part_rows, part_rows), part_rows)
@@ -165,8 +309,8 @@
         return carry
 
     lax.fori_loop(0, modes, add, 0)
-    for copy in copies:
-        copy.wait()
+    for hop in range(nt - 1):
+        finish(hop)
 
 
 def first(ns, nt, numer, probe_numer, weight):
@@ -186,7 +330,7 @@
         scratch_shapes=[
             pltpu.VMEM((ns - 1, modes, 2, part_rows, edge), F32),
             pltpu.VMEM((ns - 1, part_rows, edge), F32),
-            dma((2, nt - 1)),
+            dma((2, 2, nt - 1)),
             dma((2, ns - 1)),
             dma((2, ns - 1)),
         ],
@@ -291,50 +435,21 @@
     tile_cols = object_field.shape[2]
     pattern_count = measured.shape[0]
     edge_len = measured.shape[1]
-    mode_count = probe.shape[0]
     scan_count = lax.axis_size("scan")
     tile_count = lax.axis_size("tile")
     scan_index = lax.axis_index("scan")
     tile_index = lax.axis_index("tile")
     total_rows = strip_rows * scan_count
-    anchor = jnp.zeros((), jnp.int32)
     grid_pos = positions.reshape(scan_count, tile_count, pattern_count, 2)
-    column_pos = lax.dynamic_index_in_dim(grid_pos, tile_index, axis=1, keepdims=False)
     row_pos = lax.dynamic_index_in_dim(grid_pos, scan_index, axis=0, keepdims=False)
     row_pos = row_pos.reshape(tile_count, 2)
-    own_pos = lax.dynamic_index_in_dim(column_pos, scan_index, axis=0, keepdims=False)
-    strip = lax.all_gather(object_field, "tile", axis=2, tiled=True)
-    strip_top = scan_index * strip_rows
     tile_left = tile_index * tile_cols
-
-    power = jnp.sum(probe[:, 0] * probe[:, 0] + probe[:, 1] * probe[:, 1], axis=0)
-    all_rows = placement(positions[:, 0], strip_top, strip_rows, edge_len)
-    all_cols = placement(positions[:, 1], tile_left, tile_cols, edge_len)
-    power_all = jnp.broadcast_to(power, (positions.shape[0], 1) + power.shape)
-    denom = place_exact(power_all, all_rows, all_cols)[0]
-    denom = jnp.maximum(denom, 1.0)
-
-    def cut_slice(position):
-        row_at = position[0]
-        block_piece = lax.dynamic_slice(
-            strip, (anchor, anchor, position[1]), (2, strip_rows, edge_len)
-        )
-        intersections = jnp.logical_and(
-            strip_top < row_at + edge_len, strip_top + strip_rows > row_at
-        )
-        return jnp.where(intersections, block_piece, 0.0)
-
-    outgoing = jax.vmap(jax.vmap(cut_slice), out_axes=2)(column_pos)
-    incoming = lax.all_to_all(outgoing, "scan", split_axis=2, concat_axis=2, tiled=True)
-    column = incoming.reshape(2, total_rows, edge_len)
-    patch = lax.dynamic_slice(column, (anchor, own_pos[0, 0], anchor), (2, edge_len, edge_len))
+    patch, denom = cut(scan_count, tile_count, positions, object_field, probe)
 
     numer, probe_numer = wave(patch, probe, measured[0])
     weight = jnp.sum(patch * patch, axis=0)
 
     numers, part, weight_part = first(scan_count, tile_count, numer, probe_numer, weight)
-    sources = lax.rem(tile_index + tile_count - lax.iota(jnp.int32, tile_count), tile_count)
-    row_pos = row_pos[sources]
     row_hot = placement(row_pos[:, 0], 0, total_rows, edge_len)
     col_hot = placement(row_pos[:, 1], tile_left, tile_cols, edge_len)
     placed = place_exact(numers, row_hot, col_hot)

time: 215 us -> 183 us (0.85)
  Pallas kernels: 115 us -> 168 us
  waiting for transfers between devices: 35.2 us -> 0 us
  between operations: 14.4 us -> 0.76 us
  other arithmetic: 13.1 us -> 1.77 us
  matrix products: 14.6 us -> 3.68 us
  local copies, waits for them, and re-layouts: 16.8 us -> 8.73 us
  starting transfers between devices: 5.18 us -> 0 us
    pallas_call x0 -> x1, Pallas kernels: none -> 42.6 us  [cut(): pl.pallas_call(functools.partial(cut_kernel, ns, nt), out_shape=(jax.Shap...]
    all_gather x1 -> x0, waiting for transfers between devices: 28.4 us -> none  [body(): strip = lax.all_gather(object_field, 'tile', axis=2, tiled=True)]
    pallas_call x1, Pallas kernels: 51.4 us -> 61.5 us  [first(): pl.pallas_call(functools.partial(first_kernel, ns, nt, modes, part_rows),...]
    dot_general x2 -> x1, matrix products: 9.3 us -> 2.38 us  [place_exact(): jnp.einsum('pai,hpcaj->hcij', row_hot, both, preferred_element_type=F32)]
    all_to_all x1 -> x0, waiting for transfers between devices: 6.7 us -> none  [body(): lax.all_to_all(outgoing, 'scan', split_axis=2, concat_axis=2, tiled=True)]
    another operation x3 -> x1, other arithmetic: 6.14 us -> 0.37 us  [split_outside(): return jnp.stack([high, x - high]).astype(BF16)]
    all_to_all x1 -> x0, starting transfers between devices: 5.14 us -> none  [body(): lax.all_to_all(outgoing, 'scan', split_axis=2, concat_axis=2, tiled=True)]
    dot_general x2 -> x1, matrix products: 5.34 us -> 1.3 us  [place_exact(): jnp.einsum('hpcab,pbj->hpcaj', both, col_hot, preferred_element_type=F32)]
  transfers between devices with their start and end apart: 2 -> 0, of which waited for: 2 -> 0; matrix products, arithmetic and copies ran while one was open for 11% -> 0% of each run, Pallas kernels for 0% -> 0%
where the time goes in v3:
time: 183 us
  Pallas kernels  168 us (92%)
  local copies, waits for them, and re-layouts  8.73 us (5%)
  matrix products  3.68 us (2%)
    pallas_call x1, Pallas kernels, first(): pl.pallas_call(functools.partial(first_kernel, ns, nt, modes, part_rows),...  61.5 us
    pallas_call x1, Pallas kernels, second(): pl.pallas_call(functools.partial(second_kernel, ns, nt, own_modes, part_r...  45.3 us
    pallas_call x1, Pallas kernels, cut(): pl.pallas_call(functools.partial(cut_kernel, ns, nt), out_shape=(jax.Shap...  42.6 us
    pallas_call x1, Pallas kernels, wave(): pl.pallas_call(functools.partial(wave_kernel, edge, modes), out_shape=(ja...  18.7 us
    unnamed x13, local copies, waits for them, and re-layouts  7.34 us

profile of v3, /device:TPU:13, one launch (start us, length us, event | category | flops | bytes accessed | tf_op | source)
XLA Modules:
  0.0 183.1 jit_solution(15152979074546326764)
XLA Ops:
  0.6 0.8 reshape.17
  1.4 0.8 copy.10.positions
  2.2 0.0 copy-start
  2.2 2.2 %copy-done = f32[8,2,256,256]{3,2,1,0:T(8,128)S(1)} copy-done((f32[8,2,256,256]{3,2,1,0:T(8,128)S(1)}, f32[8,2,256,256]{3,2,1,0:T(8,128)}, u32[]{:S(2)}) %copy-start) | copy-done | bytes 4194328
  4.4 0.0 copy-start.2
  4.4 1.0 copy-done.2
  5.4 0.0 copy-start.1
  5.4 42.6 %shard_map.68 = (f32[2,256,256]{2,1,0:T(8,128)S(1)}, f32[128,512]{1,0:T(8,128)S(1)}) custom-call(s32[16,2]{1,0:T(8,128)S(1)} %copy.10.positions, f32[2,128,512]{2,1,0:T(8,128)S(1)} %copy-done.2, f32[8,2,256,256]{3,2,1,0:T(8,128)S(1)} %copy-done), custom_call_target="tpu_custom_call" | custom-call | tf_op jit(solution)/shard_map/pallas_call | solution.py:256
  48.1 0.0 copy-done.1
  48.1 0.0 copy-done.3
  48.1 0.0 copy-start.4
  48.1 1.6 copy-done.4
  49.7 18.7 %shard_map.69 = (f32[2,256,256]{2,1,0:T(8,128)S(1)}, f32[8,2,256,256]{3,2,1,0:T(8,128)S(1)}) custom-call(f32[2,256,256]{2,1,0:T(8,128)S(1)} %get-tuple-element.9.patch, f32[8,2,256,256]{3,2,1,0:T(8,128)S(1)} %copy-done.1, f32[256,256]{1,0:T(8,128)S(1)} %bitcast.34, bf16[4,512,512]{2,1,0:T(8,128)(2,1)S(1)} %copy-done.4), custom_call_target="tpu_custom_call" | custom-call | flops 12884901888 | bytes 8388608 | tf_op jit(solution)/shard_map/pallas_call | solution.py:91
  68.4 61.5 %shard_map.70 = (f32[4,2,256,256]{3,2,1,0:T(8,128)S(1)}, f32[8,2,64,256]{3,2,1,0:T(8,128)S(1)}, f32[64,256]{1,0:T(8,128)S(1)}) custom-call(f32[2,256,256]{2,1,0:T(8,128)S(1)} %get-tuple-element.10.numer, f32[8,2,256,256]{3,2,1,0:T(8,128)S(1)} %get-tuple-element.11.probe_numer, f32[256,256]{1,0:T(8,128)S(1)} %multiply_reduce_fusion.weight), custom_call_target="tpu_custom_call" | custom-call | tf_op jit(solution)/shard_map/pallas_call | solution.py:321
  129.9 0.4 fusion.10
  130.3 1.3 convolution_bitcast_fusion
  131.6 0.9 reduce-precision_convert_fusion
  132.5 2.4 %fusion.1 = f32[2,2,512,512,1]{2,3,0,1,4:T(8,128)S(1)} fusion(s32[4]{0:T(128)S(1)} %get-tuple-element.20, bf16[1,4,2,256,512]{3,4,2,0,1:T(8,128)(2,1)S(1)} %get-tuple-element.17, bf16[1,4,2,256,512]{3,4,2,0,1:T(8,128)(2,1)S(1)} %get-tuple-element.16), kind=kOutput, calls=%fused_computation.5 | convolution fusion | flops 2150629376 | bytes 8388624 | tf_op jit(solution)/shard_map/pai,hpcaj->hcij/dot_general | solution.py:429
  134.9 0.4 copy.25
  135.3 0.5 slice_add_fusion.1
  135.8 0.2 copy.26
  136.0 45.3 %shard_map.71 = (f32[2,128,512]{2,1,0:T(8,128)S(1)}, f32[2,2,256,256]{3,2,1,0:T(8,128)S(1)}) custom-call(f32[4,2,128,512]{3,2,1,0:T(8,128)S(1)} %bitcast.33, f32[128,512]{1,0:T(8,128)S(1)} %get-tuple-element.13.denom, f32[8,2,64,256]{3,2,1,0:T(8,128)S(1)} %get-tuple-element.14.part, f32[64,256]{1,0:T(8,128)S(1)} %get-tuple-element.15.weight_part), custom_call_target="tpu_custom_call" | custom-call | tf_op jit(solution)/shard_map/pallas_call | solution.py:390
  181.3 0.8 copy.29
  182.1 1.0 copy.30
  (5 shorter events, 0.1 us)
Async XLA Ops:
  2.2 2.2 %copy-start = (f32[8,2,256,256]{3,2,1,0:T(8,128)S(1)}, f32[8,2,256,256]{3,2,1,0:T(8,128)}, u32[]{:S(2)}) copy-start(f32[8,2,256,256]{3,2,1,0:T(8,128)} %probe.3) | copy-start | bytes 12582916
  4.4 1.0 copy-start.2
  5.4 42.7 %copy-start.1 = (f32[8,2,256,256]{3,2,1,0:T(8,128)S(1)}, f32[8,2,256,256]{3,2,1,0:T(8,128)}, u32[]{:S(2)}) copy-start(f32[8,2,256,256]{3,2,1,0:T(8,128)} %probe.3) | copy-start | bytes 12582916
  5.4 42.7 %copy-start.3 = (f32[1,256,256]{2,1,0:T(8,128)S(1)}, f32[1,256,256]{2,1,0:T(8,128)}, u32[]{:S(2)}) copy-start(f32[1,256,256]{2,1,0:T(8,128)} %param.7) | copy-start | bytes 786436
  48.1 1.6 copy-start.4

commit v4 on v3

--- a/solution.py
+++ b/solution.py
@@ -38,7 +38,7 @@
     return jnp.dot(a, b, preferred_element_type=F32)
 
 
-def wave_kernel(edge, modes, patch, probe, measured, tables, numer, probe_numer, far, model):
+def wave_steps(edge, modes, patch, probe, measured, tables, numer, probe_numer, far, model, done):
     fwd_h, fwd_l, inv_h, inv_l = 0, 1, 2, 3
 
     def right(x, high_at, low_at):
@@ -80,28 +80,10 @@
         numer[1] += pr * bi - pi * br
         probe_numer[k, 0] = qr * br + qi * bi
         probe_numer[k, 1] = qr * bi - qi * br
+        done(k)
         return carry
 
     lax.fori_loop(0, modes, backward, 0)
-
-
-def wave(patch, probe, measured):
-    modes, _, edge, _ = probe.shape
-    vmem = pl.BlockSpec(memory_space=pltpu.VMEM)
-    return pl.pallas_call(
-        functools.partial(wave_kernel, edge, modes),
-        out_shape=(
-            jax.ShapeDtypeStruct((2, edge, edge), F32),
-            jax.ShapeDtypeStruct((modes, 2, edge, edge), F32),
-        ),
-        in_specs=[vmem] * 4,
-        out_specs=(vmem, vmem),
-        scratch_shapes=[pltpu.VMEM((modes, 2, edge, edge), F32), pltpu.VMEM((edge, edge), F32)],
-        compiler_params=pltpu.CompilerParams(vmem_limit_bytes=40 * 2**20),
-        cost_estimate=pl.CostEstimate(
-            flops=modes * 48 * edge**3 * 2, bytes_accessed=modes * 16 * edge**2, transcendentals=0
-        ),
-    )(patch, probe, measured, jnp.asarray(dft_blocks(edge)))
 
 
 MESH = pl.DeviceIdType.MESH
@@ -275,36 +257,86 @@
     )(positions, tile_block, probe)
 
 
+def row_block(ns, scan, part_rows):
+    at = lax.rem(scan, 2) * (ns // 2) + scan // 2
+    return pl.ds(pl.multiple_of(at * part_rows, part_rows), part_rows)
+
+
 def first_kernel(
-    ns, nt, modes, part_rows, numer, probe_numer, weight, numers, part, weight_part, got, got_w, z_sems, p_sems, w_sems
+    ns, nt, modes, part_rows, patch, probe, measured, tables, numers, part, weight_part,
+    far, model, numer, probe_numer, weight, got_c, half, got_x, got_w,
+    z_sems, c_sems, x_sems, w_sems,
 ):
     scan, tile = lax.axis_index("scan"), lax.axis_index("tile")
+    core, column, nx = lax.rem(scan, 2), scan // 2, ns // 2
+    edge = patch.shape[1]
+    half_rows = nx * part_rows
     greet((("scan", ns), ("tile", nt)))
+    weight[...] = patch[0] * patch[0] + patch[1] * patch[1]
+    weights = []
+    for i in range(1, ns):
+        peer = lax.rem(scan + i, ns)
+        rows = weight.at[row_block(ns, peer, part_rows), :]
+        weights.append(push(rows, got_w.at[i - 1], w_sems, i - 1, "scan", peer))
+
+    def to_core(k):
+        rows = pl.ds(pl.multiple_of((1 - core) * half_rows, half_rows), half_rows)
+        return pltpu.make_async_remote_copy(
+            src_ref=probe_numer.at[k, :, rows, :],
+            dst_ref=got_c.at[k],
+            send_sem=c_sems.at[0, k],
+            recv_sem=c_sems.at[1, k],
+            device_id={"scan": scan + 1 - 2 * core},
+            device_id_type=MESH,
+        )
+
+    def to_chip(k, i):
+        peer = lax.rem(column + i, nx)
+        rows = pl.ds(pl.multiple_of(peer * part_rows, part_rows), part_rows)
+        return pltpu.make_async_remote_copy(
+            src_ref=half.at[k, :, rows, :],
+            dst_ref=got_x.at[i - 1, k],
+            send_sem=x_sems.at[0, i - 1, k],
+            recv_sem=x_sems.at[1, i - 1, k],
+            device_id={"scan": peer * 2 + core},
+            device_id_type=MESH,
+        )
+
+    def pass_on(k):
+        to_core(k).wait()
+        rows = pl.ds(pl.multiple_of(core * half_rows, half_rows), half_rows)
+        half[k] = probe_numer[k, :, rows, :] + got_c[k]
+        for i in range(1, nx):
+            to_chip(k, i).start()
+
+    def done(k):
+        to_core(k).start()
+        pl.when(k >= 2)(lambda: pass_on(jnp.maximum(k - 2, 0)))
+
+    wave_steps(edge, modes, patch, probe, measured, tables, numer, probe_numer, far, model, done)
     numers[tile] = numer[...]
     start, receive, finish = relay(nt, numers, z_sems)
     start(0)
-    sums = []
-    for i in range(1, ns):
-        peer = lax.rem(scan + i, ns)
-        span = pl.ds(pl.multiple_of(peer * part_rows, part_rows), part_rows)
-        sums.append(push(weight.at[span, :], got_w.at[i - 1], w_sems, i - 1, "scan", peer))
-        sums.append(push(probe_numer.at[:, :, span, :], got.at[i - 1], p_sems, i - 1, "scan", peer))
+    for k in range(max(modes - 2, 0), modes):
+        pass_on(k)
     for hop in range(nt - 1):
         receive(hop)
         if hop + 1 < nt - 1:
             start(hop + 1)
-    for copy in sums:
+    for copy in weights:
         copy.wait()
-    mine = pl.ds(pl.multiple_of(scan * part_rows, part_rows), part_rows)
-    total = weight[mine, :]
+    total = weight[row_block(ns, scan, part_rows), :]
     for i in range(ns - 1):
         total += got_w[i]
     weight_part[...] = total
 
     def add(k, carry):
-        value = probe_numer[k, :, mine, :]
-        for i in range(ns - 1):
-            value += got[i, k]
+        rows = pl.ds(pl.multiple_of(column * part_rows, part_rows), part_rows)
+        for i in range(1, nx):
+            to_chip(k, i).wait()
+        value = half[k, :, rows, :]
+        for i in range(nx - 1):
+            value += got_x[i, k]
         part[k] = value
         return carry
 
@@ -313,9 +345,11 @@
         finish(hop)
 
 
-def first(ns, nt, numer, probe_numer, weight):
-    modes, _, edge, _ = probe_numer.shape
+def first(ns, nt, patch, probe, measured):
+    modes, _, edge, _ = probe.shape
     part_rows = edge // ns
+    nx = ns // 2
+    half_rows = nx * part_rows
     vmem = pl.BlockSpec(memory_space=pltpu.VMEM)
     dma = pltpu.SemaphoreType.DMA
     return pl.pallas_call(
@@ -325,19 +359,27 @@
             jax.ShapeDtypeStruct((modes, 2, part_rows, edge), F32),
             jax.ShapeDtypeStruct((part_rows, edge), F32),
         ),
-        in_specs=[vmem] * 3,
+        in_specs=[vmem] * 4,
         out_specs=(vmem,) * 3,
         scratch_shapes=[
-            pltpu.VMEM((ns - 1, modes, 2, part_rows, edge), F32),
+            pltpu.VMEM((modes, 2, edge, edge), F32),
+            pltpu.VMEM((edge, edge), F32),
+            pltpu.VMEM((2, edge, edge), F32),
+            pltpu.VMEM((modes, 2, edge, edge), F32),
+            pltpu.VMEM((edge, edge), F32),
+            pltpu.VMEM((modes, 2, half_rows, edge), F32),
+            pltpu.VMEM((modes, 2, half_rows, edge), F32),
+            pltpu.VMEM((nx - 1, modes, 2, part_rows, edge), F32),
             pltpu.VMEM((ns - 1, part_rows, edge), F32),
             dma((2, 2, nt - 1)),
-            dma((2, ns - 1)),
+            dma((2, modes)),
+            dma((2, nx - 1, modes)),
             dma((2, ns - 1)),
         ],
         compiler_params=pltpu.CompilerParams(
-            collective_id=0, has_side_effects=True, vmem_limit_bytes=40 * 2**20
-        ),
-    )(numer, probe_numer, weight)
+            collective_id=0, has_side_effects=True, vmem_limit_bytes=48 * 2**20
+        ),
+    )(patch, probe, measured, jnp.asarray(dft_blocks(edge)))
 
 
 def second_kernel(
@@ -360,7 +402,7 @@
     for i in range(nt - 1):
         total += got_w[i]
     scale = 1.0 / (total + 1e-05)
-    mine = pl.ds(pl.multiple_of(scan * part_rows, part_rows), part_rows)
+    mine = row_block(ns, scan, part_rows)
     for k in range(own_modes):
         value = part[tile * own_modes + k]
         for i in range(nt - 1):
@@ -446,10 +488,7 @@
     tile_left = tile_index * tile_cols
     patch, denom = cut(scan_count, tile_count, positions, object_field, probe)
 
-    numer, probe_numer = wave(patch, probe, measured[0])
-    weight = jnp.sum(patch * patch, axis=0)
-
-    numers, part, weight_part = first(scan_count, tile_count, numer, probe_numer, weight)
+    numers, part, weight_part = first(scan_count, tile_count, patch, probe, measured[0])
     row_hot = placement(row_pos[:, 0], 0, total_rows, edge_len)
     col_hot = placement(row_pos[:, 1], tile_left, tile_cols, edge_len)
     placed = place_exact(numers, row_hot, col_hot)

time: 183 us -> 174 us (0.951)
  Pallas kernels: 168 us -> 160 us
    pallas_call x1 -> x0, Pallas kernels: 18.7 us -> none  [wave(): pl.pallas_call(functools.partial(wave_kernel, edge, modes), out_shape=(ja...]
    pallas_call x1, Pallas kernels: 61.5 us -> 68.8 us  [first(): pl.pallas_call(functools.partial(first_kernel, ns, nt, modes, part_rows),...]
    pallas_call x1, Pallas kernels: 45.3 us -> 48.8 us  [second(): pl.pallas_call(functools.partial(second_kernel, ns, nt, own_modes, part_r...]
    unnamed x13 -> x11, local copies, waits for them, and re-layouts: 7.34 us -> 5.76 us
where the time goes in v4:
time: 174 us
  Pallas kernels  160 us (92%)
  local copies, waits for them, and re-layouts  7.15 us (4%)
  matrix products  3.68 us (2%)
    pallas_call x1, Pallas kernels, first(): pl.pallas_call(functools.partial(first_kernel, ns, nt, modes, part_rows),...  68.8 us
    pallas_call x1, Pallas kernels, second(): pl.pallas_call(functools.partial(second_kernel, ns, nt, own_modes, part_r...  48.8 us
    pallas_call x1, Pallas kernels, cut(): pl.pallas_call(functools.partial(cut_kernel, ns, nt), out_shape=(jax.Shap...  42.6 us
    unnamed x11, local copies, waits for them, and re-layouts  5.76 us

profile of v4, /device:TPU:13, one launch (start us, length us, event | category | flops | bytes accessed | tf_op | source)
XLA Modules:
  0.0 173.6 jit_solution(13760241505824030587)
XLA Ops:
  0.6 0.8 reshape.17
  1.4 0.8 copy.10.positions
  2.2 0.0 copy-start
  2.2 2.2 %copy-done = f32[8,2,256,256]{3,2,1,0:T(8,128)S(1)} copy-done((f32[8,2,256,256]{3,2,1,0:T(8,128)S(1)}, f32[8,2,256,256]{3,2,1,0:T(8,128)}, u32[]{:S(2)}) %copy-start) | copy-done | bytes 4194328
  4.4 0.0 copy-start.2
  4.4 1.0 copy-done.2
  5.4 0.0 copy-start.1
  5.4 0.0 copy-start.3
  5.4 42.6 %shard_map.68 = (f32[2,256,256]{2,1,0:T(8,128)S(1)}, f32[128,512]{1,0:T(8,128)S(1)}) custom-call(s32[16,2]{1,0:T(8,128)S(1)} %copy.10.positions, f32[2,128,512]{2,1,0:T(8,128)S(1)} %copy-done.2, f32[8,2,256,256]{3,2,1,0:T(8,128)S(1)} %copy-done), custom_call_target="tpu_custom_call" | custom-call | tf_op jit(solution)/shard_map/pallas_call | solution.py:238
  48.1 0.0 copy-done.1
  48.1 0.0 copy-done.3
  48.1 68.8 %shard_map.69 = (f32[4,2,256,256]{3,2,1,0:T(8,128)S(1)}, f32[8,2,64,256]{3,2,1,0:T(8,128)S(1)}, f32[64,256]{1,0:T(8,128)S(1)}) custom-call(f32[2,256,256]{2,1,0:T(8,128)S(1)} %get-tuple-element.7.patch, f32[8,2,256,256]{3,2,1,0:T(8,128)} %probe.3, f32[256,256]{1,0:T(8,128)S(1)} %bitcast.34, bf16[4,512,512]{2,1,0:T(8,128)(2,1)S(1)} %copy-done.1), custom_call_target="tpu_custom_call" | custom-call | tf_op jit(solution)/shard_map/pallas_call | solution.py:355
  116.9 0.4 fusion.10
  117.3 1.3 convolution_bitcast_fusion
  118.6 0.9 reduce-precision_convert_fusion
  119.5 2.4 %fusion.1 = f32[2,2,512,512,1]{2,3,0,1,4:T(8,128)S(1)} fusion(s32[4]{0:T(128)S(1)} %get-tuple-element.16, bf16[1,4,2,256,512]{3,4,2,0,1:T(8,128)(2,1)S(1)} %get-tuple-element.13, bf16[1,4,2,256,512]{3,4,2,0,1:T(8,128)(2,1)S(1)} %get-tuple-element.12), kind=kOutput, calls=%fused_computation.5 | convolution fusion | flops 2150629376 | bytes 8388624 | tf_op jit(solution)/shard_map/pai,hpcaj->hcij/dot_general | solution.py:471
  121.8 0.4 copy.25
  122.3 0.5 slice_add_fusion.1
  122.8 0.2 copy.26
  123.0 48.8 %shard_map.70 = (f32[2,128,512]{2,1,0:T(8,128)S(1)}, f32[2,2,256,256]{3,2,1,0:T(8,128)S(1)}) custom-call(f32[4,2,128,512]{3,2,1,0:T(8,128)S(1)} %bitcast.33, f32[128,512]{1,0:T(8,128)S(1)} %get-tuple-element.9.denom, f32[8,2,64,256]{3,2,1,0:T(8,128)S(1)} %get-tuple-element.10.part, f32[64,256]{1,0:T(8,128)S(1)} %get-tuple-element.11.weight_part), custom_call_target="tpu_custom_call" | custom-call | tf_op jit(solution)/shard_map/pallas_call | solution.py:432
  171.8 0.8 copy.29
  172.6 1.0 copy.30
  (3 shorter events, 0.0 us)
Async XLA Ops:
  2.2 2.2 %copy-start = (f32[8,2,256,256]{3,2,1,0:T(8,128)S(1)}, f32[8,2,256,256]{3,2,1,0:T(8,128)}, u32[]{:S(2)}) copy-start(f32[8,2,256,256]{3,2,1,0:T(8,128)} %probe.3) | copy-start | bytes 12582916
  4.4 1.0 copy-start.2
  5.4 42.7 %copy-start.1 = (bf16[4,512,512]{2,1,0:T(8,128)(2,1)S(1)}, bf16[4,512,512]{2,1,0:T(8,128)(2,1)}, u32[]{:S(2)}) copy-start(bf16[4,512,512]{2,1,0:T(8,128)(2,1)} %constant.17.clone.tables) | copy-start | bytes 6291460
  5.4 42.7 %copy-start.3 = (f32[1,256,256]{2,1,0:T(8,128)S(1)}, f32[1,256,256]{2,1,0:T(8,128)}, u32[]{:S(2)}) copy-start(f32[1,256,256]{2,1,0:T(8,128)} %param.7) | copy-start | bytes 786436

commit v5 on v4

--- a/solution.py
+++ b/solution.py
@@ -118,34 +118,49 @@
 def relay(nt, slots, sems):
     tile = lax.axis_index("tile")
 
-    def copy(slot, way, hop, peer):
+    def copy(slot, way, hop, peer, c):
         at = jnp.clip(slot, 0, nt - 1)
         return pltpu.make_async_remote_copy(
-            src_ref=slots.at[at],
-            dst_ref=slots.at[at],
-            send_sem=sems.at[0, way, hop],
-            recv_sem=sems.at[1, way, hop],
+            src_ref=slots.at[at, c],
+            dst_ref=slots.at[at, c],
+            send_sem=sems.at[0, way, hop, c],
+            recv_sem=sems.at[1, way, hop, c],
             device_id={"tile": jnp.clip(peer, 0, nt - 1)},
             device_id_type=MESH,
         )
 
-    def sends(hop, act):
+    def send_up(hop, c, act):
         pl.when(jnp.logical_and(tile + 1 < nt, tile - hop >= 0))(
-            lambda: act(copy(tile - hop, 0, hop, tile + 1))
+            lambda: act(copy(tile - hop, 0, hop, tile + 1, c))
         )
+
+    def send_down(hop, c, act):
         pl.when(jnp.logical_and(tile - 1 >= 0, tile + hop < nt))(
-            lambda: act(copy(tile + hop, 1, hop, tile - 1))
+            lambda: act(copy(tile + hop, 1, hop, tile - 1, c))
         )
 
     def start(hop):
-        sends(hop, lambda c: c.start())
+        for c in range(2):
+            send_up(hop, c, lambda d: d.start())
+            send_down(hop, c, lambda d: d.start())
 
     def finish(hop):
-        sends(hop, lambda c: c.wait_send())
+        for c in range(2):
+            send_up(hop, c, lambda d: d.wait_send())
+            send_down(hop, c, lambda d: d.wait_send())
 
     def receive(hop):
-        pl.when(tile - 1 - hop >= 0)(lambda: copy(tile - 1 - hop, 0, hop, tile - 1).wait_recv())
-        pl.when(tile + 1 + hop < nt)(lambda: copy(tile + 1 + hop, 1, hop, tile + 1).wait_recv())
+        for c in range(2):
+            pl.when(tile - 1 - hop >= 0)(
+                lambda: copy(tile - 1 - hop, 0, hop, tile - 1, c).wait_recv()
+            )
+            if hop + 1 < nt - 1:
+                send_up(hop + 1, c, lambda d: d.start())
+            pl.when(tile + 1 + hop < nt)(
+                lambda: copy(tile + 1 + hop, 1, hop, tile + 1, c).wait_recv()
+            )
+            if hop + 1 < nt - 1:
+                send_down(hop + 1, c, lambda d: d.start())
 
     return start, receive, finish
 
@@ -203,8 +218,6 @@
     denom[...] = jnp.maximum(denom[...], 1.0)
     for hop in range(nt - 1):
         receive(hop)
-        if hop + 1 < nt - 1:
-            start(hop + 1)
         pl.when(tile - 1 - hop >= 0)(lambda: cut(jnp.maximum(tile - 1 - hop, 0)))
         pl.when(tile + 1 + hop < nt)(lambda: cut(jnp.minimum(tile + 1 + hop, nt - 1)))
     copies = []
@@ -248,7 +261,7 @@
             pltpu.VMEM((ns, 2, strip_rows, edge), F32),
             pltpu.VMEM((ns - 1, 2, strip_rows, edge), F32),
             pltpu.VMEM((edge, edge), F32),
-            dma((2, 2, nt - 1)),
+            dma((2, 2, nt - 1, 2)),
             dma((2, ns - 1)),
         ],
         compiler_params=pltpu.CompilerParams(
@@ -321,8 +334,6 @@
         pass_on(k)
     for hop in range(nt - 1):
         receive(hop)
-        if hop + 1 < nt - 1:
-            start(hop + 1)
     for copy in weights:
         copy.wait()
     total = weight[row_block(ns, scan, part_rows), :]
@@ -371,7 +382,7 @@
             pltpu.VMEM((modes, 2, half_rows, edge), F32),
             pltpu.VMEM((nx - 1, modes, 2, part_rows, edge), F32),
             pltpu.VMEM((ns - 1, part_rows, edge), F32),
-            dma((2, 2, nt - 1)),
+            dma((2, 2, nt - 1, 2)),
             dma((2, modes)),
             dma((2, nx - 1, modes)),
             dma((2, ns - 1)),
@@ -383,7 +394,7 @@
 
 
 def second_kernel(
-    ns, nt, own_modes, part_rows, placed, denom, part, weight_part, grad, probe_grad, got_o, got_p, got_w, o_sems, p_sems, w_sems, g_sems
+    ns, nt, own_modes, part_rows, positions, numers, denom, part, weight_part, grad, probe_grad, placed, cols_h, cols_l, got_o, got_p, got_w, o_sems, p_sems, w_sems, g_sems
 ):
     scan, tile = lax.axis_index("scan"), lax.axis_index("tile")
     greet((("scan", ns), ("tile", nt)))
@@ -393,9 +404,35 @@
         span = pl.ds(peer * own_modes, own_modes)
         probe_copies.append(push(weight_part, got_w.at[i - 1], w_sems, i - 1, "tile", peer))
         probe_copies.append(push(part.at[span], got_p.at[i - 1], p_sems, i - 1, "tile", peer))
+    strip_rows, tile_cols = denom.shape
+    edge = numers.shape[2]
+
+    def columns(o, carry):
+        pick = hot((edge, tile_cols), positions[scan * nt + o, 1], tile * tile_cols)
+        high, low = split(numers[o].reshape(2 * edge, edge))
+        high, low = split((dot(high, pick) + dot(low, pick)).reshape(2, edge, tile_cols))
+        cols_h[o] = high
+        cols_l[o] = low
+        return carry
+
+    lax.fori_loop(0, nt, columns, 0)
+
+    def place(dest):
+        placed[dest] = jnp.zeros((2, strip_rows, tile_cols), F32)
+
+        def one(o, carry):
+            pick = hot((strip_rows, edge), dest * strip_rows, positions[scan * nt + o, 0])
+            for c in range(2):
+                placed[dest, c] += dot(pick, cols_h[o, c]) + dot(pick, cols_l[o, c])
+            return carry
+
+        lax.fori_loop(0, nt, one, 0)
+
     for i in range(1, ns):
         peer = lax.rem(scan + i, ns)
+        place(peer)
         object_copies.append(push(placed.at[peer], got_o.at[i - 1], o_sems, i - 1, "scan", peer))
+    place(scan)
     for copy in probe_copies:
         copy.wait()
     total = weight_part[...]
@@ -423,10 +460,10 @@
         copy.wait()
 
 
-def second(ns, nt, placed, denom, part, weight_part):
+def second(ns, nt, positions, numers, denom, part, weight_part):
     modes, _, part_rows, edge = part.shape
     own_modes = modes // nt
-    block = placed.shape[1:]
+    block = (2,) + denom.shape
     vmem = pl.BlockSpec(memory_space=pltpu.VMEM)
     dma = pltpu.SemaphoreType.DMA
     return pl.pallas_call(
@@ -435,9 +472,12 @@
             jax.ShapeDtypeStruct(block, F32),
             jax.ShapeDtypeStruct((own_modes, 2, edge, edge), F32),
         ),
-        in_specs=[vmem] * 4,
+        in_specs=[pl.BlockSpec(memory_space=pltpu.SMEM)] + [vmem] * 4,
         out_specs=(vmem,) * 2,
         scratch_shapes=[
+            pltpu.VMEM((ns,) + block, F32),
+            pltpu.VMEM((nt, 2, edge, denom.shape[1]), BF16),
+            pltpu.VMEM((nt, 2, edge, denom.shape[1]), BF16),
             pltpu.VMEM((ns - 1,) + block, F32),
             pltpu.VMEM((nt - 1, own_modes, 2, part_rows, edge), F32),
             pltpu.VMEM((nt - 1, part_rows, edge), F32),
@@ -449,52 +489,17 @@
         compiler_params=pltpu.CompilerParams(
             collective_id=1, has_side_effects=True, vmem_limit_bytes=40 * 2**20
         ),
-    )(placed, denom, part, weight_part)
-
-
-def placement(start, offset, size, edge):
-    at = start[:, None, None] + lax.broadcasted_iota(jnp.int32, (1, edge, size), 1)
-    here = offset + lax.broadcasted_iota(jnp.int32, (1, edge, size), 2)
-    return (at == here).astype(BF16)
-
-
-def split_outside(x):
-    high = lax.reduce_precision(x, 8, 7)
-    return jnp.stack([high, x - high]).astype(BF16)
-
-
-def place_exact(images, row_hot, col_hot):
-    both = split_outside(images)
-    cols = jnp.einsum("hpcab,pbj->hpcaj", both, col_hot, preferred_element_type=F32)
-    cols = cols[0] + cols[1]
-    both = split_outside(cols)
-    out = jnp.einsum("pai,hpcaj->hcij", row_hot, both, preferred_element_type=F32)
-    return out[0] + out[1]
+    )(positions, numers, denom, part, weight_part)
 
 
 def body(object_field, probe, measured, positions):
-    strip_rows = object_field.shape[1]
-    tile_cols = object_field.shape[2]
-    pattern_count = measured.shape[0]
-    edge_len = measured.shape[1]
     scan_count = lax.axis_size("scan")
     tile_count = lax.axis_size("tile")
-    scan_index = lax.axis_index("scan")
-    tile_index = lax.axis_index("tile")
-    total_rows = strip_rows * scan_count
-    grid_pos = positions.reshape(scan_count, tile_count, pattern_count, 2)
-    row_pos = lax.dynamic_index_in_dim(grid_pos, scan_index, axis=0, keepdims=False)
-    row_pos = row_pos.reshape(tile_count, 2)
-    tile_left = tile_index * tile_cols
     patch, denom = cut(scan_count, tile_count, positions, object_field, probe)
 
     numers, part, weight_part = first(scan_count, tile_count, patch, probe, measured[0])
-    row_hot = placement(row_pos[:, 0], 0, total_rows, edge_len)
-    col_hot = placement(row_pos[:, 1], tile_left, tile_cols, edge_len)
-    placed = place_exact(numers, row_hot, col_hot)
-    placed = placed.reshape(2, scan_count, strip_rows, tile_cols).transpose(1, 0, 2, 3)
     object_gradient, probe_gradient = second(
-        scan_count, tile_count, placed, denom, part, weight_part
+        scan_count, tile_count, positions, numers, denom, part, weight_part
     )
     return (object_gradient, probe_gradient)
 

time: 174 us -> 162 us (0.931)
  Pallas kernels: 160 us -> 155 us
  matrix products: 3.68 us -> 0 us
    dot_general x2 -> x0, matrix products: 3.68 us -> none  [the longest x1 2.38 us: place_exact(): jnp.einsum('pai,hpcaj->hcij', row_hot, both, preferred_element_type=F32)]
    pallas_call x1, Pallas kernels: 48.8 us -> 45.7 us  [second(): pl.pallas_call(functools.partial(second_kernel, ns, nt, own_modes, part_r...]
where the time goes in v5:
time: 162 us
  Pallas kernels  155 us (96%)
  local copies, waits for them, and re-layouts  5.76 us (4%)
    pallas_call x1, Pallas kernels, first(): pl.pallas_call(functools.partial(first_kernel, ns, nt, modes, part_rows),...  68.1 us
    pallas_call x1, Pallas kernels, second(): pl.pallas_call(functools.partial(second_kernel, ns, nt, own_modes, part_r...  45.7 us
    pallas_call x1, Pallas kernels, cut(): pl.pallas_call(functools.partial(cut_kernel, ns, nt), out_shape=(jax.Shap...  41.5 us
    unnamed x11, local copies, waits for them, and re-layouts  5.76 us

profile of v5, /device:TPU:13, one launch (start us, length us, event | category | flops | bytes accessed | tf_op | source)
XLA Modules:
  0.0 161.8 jit_solution(11538648784089531342)
XLA Ops:
  0.6 0.8 copy.8.positions
  1.4 0.0 copy-start
  1.4 2.2 %copy-done = f32[8,2,256,256]{3,2,1,0:T(8,128)S(1)} copy-done((f32[8,2,256,256]{3,2,1,0:T(8,128)S(1)}, f32[8,2,256,256]{3,2,1,0:T(8,128)}, u32[]{:S(2)}) %copy-start) | copy-done | bytes 4194328
  3.6 0.0 copy-start.2
  3.6 1.0 copy-done.2
  4.6 0.0 copy-start.1
  4.6 0.0 copy-start.3
  4.6 41.5 %shard_map.68 = (f32[2,256,256]{2,1,0:T(8,128)S(1)}, f32[128,512]{1,0:T(8,128)S(1)}) custom-call(s32[16,2]{1,0:T(8,128)S(1)} %copy.8.positions, f32[2,128,512]{2,1,0:T(8,128)S(1)} %copy-done.2, f32[8,2,256,256]{3,2,1,0:T(8,128)S(1)} %copy-done), custom_call_target="tpu_custom_call" | custom-call | tf_op jit(solution)/shard_map/pallas_call | solution.py:251
  46.1 0.0 copy-done.1
  46.1 0.0 copy-done.3
  46.2 68.1 %shard_map.69 = (f32[4,2,256,256]{3,2,1,0:T(8,128)S(1)}, f32[8,2,64,256]{3,2,1,0:T(8,128)S(1)}, f32[64,256]{1,0:T(8,128)S(1)}) custom-call(f32[2,256,256]{2,1,0:T(8,128)S(1)} %get-tuple-element.7.patch, f32[8,2,256,256]{3,2,1,0:T(8,128)} %probe.3, f32[256,256]{1,0:T(8,128)S(1)} %bitcast.1, bf16[4,512,512]{2,1,0:T(8,128)(2,1)S(1)} %copy-done.1), custom_call_target="tpu_custom_call" | custom-call | tf_op jit(solution)/shard_map/pallas_call | solution.py:366
  114.3 45.7 %shard_map.70 = (f32[2,128,512]{2,1,0:T(8,128)S(1)}, f32[2,2,256,256]{3,2,1,0:T(8,128)S(1)}) custom-call(s32[16,2]{1,0:T(8,128)S(1)} %copy.8.positions, f32[4,2,256,256]{3,2,1,0:T(8,128)S(1)} %get-tuple-element.8.numers, f32[128,512]{1,0:T(8,128)S(1)} %get-tuple-element.9.denom, f32[8,2,64,256]{3,2,1,0:T(8,128)S(1)} %get-tuple-element.10.part, ...), custom_call_target="tpu_custom_call" | custom-call | tf_op jit(solution)/shard_map/pallas_call | solution.py:469
  160.1 0.8 copy.11
  160.9 1.0 copy.12
Async XLA Ops:
  1.4 2.2 %copy-start = (f32[8,2,256,256]{3,2,1,0:T(8,128)S(1)}, f32[8,2,256,256]{3,2,1,0:T(8,128)}, u32[]{:S(2)}) copy-start(f32[8,2,256,256]{3,2,1,0:T(8,128)} %probe.3) | copy-start | bytes 12582916
  3.6 1.0 copy-start.2
  4.6 41.5 %copy-start.1 = (bf16[4,512,512]{2,1,0:T(8,128)(2,1)S(1)}, bf16[4,512,512]{2,1,0:T(8,128)(2,1)}, u32[]{:S(2)}) copy-start(bf16[4,512,512]{2,1,0:T(8,128)(2,1)} %constant.2.clone.tables) | copy-start | bytes 6291460
  4.6 41.5 %copy-start.3 = (f32[1,256,256]{2,1,0:T(8,128)S(1)}, f32[1,256,256]{2,1,0:T(8,128)}, u32[]{:S(2)}) copy-start(f32[1,256,256]{2,1,0:T(8,128)} %param.7) | copy-start | bytes 786436

commit v6 on v5

--- a/solution.py
+++ b/solution.py
@@ -394,7 +394,7 @@
 
 
 def second_kernel(
-    ns, nt, own_modes, part_rows, positions, numers, denom, part, weight_part, grad, probe_grad, placed, cols_h, cols_l, got_o, got_p, got_w, o_sems, p_sems, w_sems, g_sems
+    ns, nt, own_modes, part_rows, positions, numers, denom, part, weight_part, grad, probe_grad, placed, cols_h, cols_l, got_c, got_o, got_p, got_w, c_sems, o_sems, p_sems, w_sems, g_sems
 ):
     scan, tile = lax.axis_index("scan"), lax.axis_index("tile")
     greet((("scan", ns), ("tile", nt)))
@@ -428,11 +428,22 @@
 
         lax.fori_loop(0, nt, one, 0)
 
-    for i in range(1, ns):
-        peer = lax.rem(scan + i, ns)
-        place(peer)
+    core, column, nx = lax.rem(scan, 2), scan // 2, ns // 2
+    core_copies = []
+    for p in range(nx):
+        dest = p * 2 + 1 - core
+        place(dest)
+        core_copies.append(
+            push(placed.at[dest], got_c.at[p], c_sems, p, "scan", scan + 1 - 2 * core)
+        )
+    for p in range(nx):
+        place(p * 2 + core)
+    for p in range(nx):
+        core_copies[p].wait()
+        placed[p * 2 + core] += got_c[p]
+    for i in range(1, nx):
+        peer = lax.rem(column + i, nx) * 2 + core
         object_copies.append(push(placed.at[peer], got_o.at[i - 1], o_sems, i - 1, "scan", peer))
-    place(scan)
     for copy in probe_copies:
         copy.wait()
     total = weight_part[...]
@@ -453,7 +464,7 @@
         copy.wait()
     for c in range(2):
         value = placed[scan, c]
-        for i in range(ns - 1):
+        for i in range(nx - 1):
             value += got_o[i, c]
         grad[c] = value / denom[...]
     for copy in last:
@@ -478,10 +489,12 @@
             pltpu.VMEM((ns,) + block, F32),
             pltpu.VMEM((nt, 2, edge, denom.shape[1]), BF16),
             pltpu.VMEM((nt, 2, edge, denom.shape[1]), BF16),
-            pltpu.VMEM((ns - 1,) + block, F32),
+            pltpu.VMEM((ns // 2,) + block, F32),
+            pltpu.VMEM((ns // 2 - 1,) + block, F32),
             pltpu.VMEM((nt - 1, own_modes, 2, part_rows, edge), F32),
             pltpu.VMEM((nt - 1, part_rows, edge), F32),
-            dma((2, ns - 1)),
+            dma((2, ns // 2)),
+            dma((2, ns // 2 - 1)),
             dma((2, nt - 1)),
             dma((2, nt - 1)),
             dma((2, ns - 1)),

time: 162 us -> 162 us (level)
  no operation moved by 1% of the time
where the time goes in v6:
time: 162 us
  Pallas kernels  155 us (96%)
  local copies, waits for them, and re-layouts  5.76 us (4%)
    pallas_call x1, Pallas kernels, first(): pl.pallas_call(functools.partial(first_kernel, ns, nt, modes, part_rows),...  68.1 us
    pallas_call x1, Pallas kernels, second(): pl.pallas_call(functools.partial(second_kernel, ns, nt, own_modes, part_r...  45.7 us
    pallas_call x1, Pallas kernels, cut(): pl.pallas_call(functools.partial(cut_kernel, ns, nt), out_shape=(jax.Shap...  41.5 us
    unnamed x11, local copies, waits for them, and re-layouts  5.76 us

profile of v6, /device:TPU:13, one launch (start us, length us, event | category | flops | bytes accessed | tf_op | source)
XLA Modules:
  0.0 161.8 jit_solution(6951890025472198933)
XLA Ops:
  0.6 0.8 copy.8.positions
  1.4 0.0 copy-start
  1.4 2.2 %copy-done = f32[8,2,256,256]{3,2,1,0:T(8,128)S(1)} copy-done((f32[8,2,256,256]{3,2,1,0:T(8,128)S(1)}, f32[8,2,256,256]{3,2,1,0:T(8,128)}, u32[]{:S(2)}) %copy-start) | copy-done | bytes 4194328
  3.6 0.0 copy-start.2
  3.6 1.0 copy-done.2
  4.6 0.0 copy-start.1
  4.6 0.0 copy-start.3
  4.6 41.5 %shard_map.68 = (f32[2,256,256]{2,1,0:T(8,128)S(1)}, f32[128,512]{1,0:T(8,128)S(1)}) custom-call(s32[16,2]{1,0:T(8,128)S(1)} %copy.8.positions, f32[2,128,512]{2,1,0:T(8,128)S(1)} %copy-done.2, f32[8,2,256,256]{3,2,1,0:T(8,128)S(1)} %copy-done), custom_call_target="tpu_custom_call" | custom-call | tf_op jit(solution)/shard_map/pallas_call | solution.py:251
  46.1 0.0 copy-done.1
  46.1 0.0 copy-done.3
  46.2 68.1 %shard_map.69 = (f32[4,2,256,256]{3,2,1,0:T(8,128)S(1)}, f32[8,2,64,256]{3,2,1,0:T(8,128)S(1)}, f32[64,256]{1,0:T(8,128)S(1)}) custom-call(f32[2,256,256]{2,1,0:T(8,128)S(1)} %get-tuple-element.7.patch, f32[8,2,256,256]{3,2,1,0:T(8,128)} %probe.3, f32[256,256]{1,0:T(8,128)S(1)} %bitcast.1, bf16[4,512,512]{2,1,0:T(8,128)(2,1)S(1)} %copy-done.1), custom_call_target="tpu_custom_call" | custom-call | tf_op jit(solution)/shard_map/pallas_call | solution.py:366
  114.3 45.7 %shard_map.70 = (f32[2,128,512]{2,1,0:T(8,128)S(1)}, f32[2,2,256,256]{3,2,1,0:T(8,128)S(1)}) custom-call(s32[16,2]{1,0:T(8,128)S(1)} %copy.8.positions, f32[4,2,256,256]{3,2,1,0:T(8,128)S(1)} %get-tuple-element.8.numers, f32[128,512]{1,0:T(8,128)S(1)} %get-tuple-element.9.denom, f32[8,2,64,256]{3,2,1,0:T(8,128)S(1)} %get-tuple-element.10.part, ...), custom_call_target="tpu_custom_call" | custom-call | tf_op jit(solution)/shard_map/pallas_call | solution.py:480
  160.1 0.8 copy.11
  160.9 1.0 copy.12
Async XLA Ops:
  1.4 2.2 %copy-start = (f32[8,2,256,256]{3,2,1,0:T(8,128)S(1)}, f32[8,2,256,256]{3,2,1,0:T(8,128)}, u32[]{:S(2)}) copy-start(f32[8,2,256,256]{3,2,1,0:T(8,128)} %probe.3) | copy-start | bytes 12582916
  3.6 1.0 copy-start.2
  4.6 41.5 %copy-start.1 = (bf16[4,512,512]{2,1,0:T(8,128)(2,1)S(1)}, bf16[4,512,512]{2,1,0:T(8,128)(2,1)}, u32[]{:S(2)}) copy-start(bf16[4,512,512]{2,1,0:T(8,128)(2,1)} %constant.2.clone.tables) | copy-start | bytes 6291460
  4.6 41.5 %copy-start.3 = (f32[1,256,256]{2,1,0:T(8,128)S(1)}, f32[1,256,256]{2,1,0:T(8,128)}, u32[]{:S(2)}) copy-start(f32[1,256,256]{2,1,0:T(8,128)} %param.7) | copy-start | bytes 786436
